TPU v7x, 32 devices: a whole 2x2x4 slice. The times are simulated.
32 devices in a mesh: replica: 2 (over x), fsdp: 16 (over z, y, core).
Axes of the slice: x: 2, y: 2, z: 4, core: 2. Of those that a mesh axis runs over, the one named last changes fastest.
Arguments:
- tokens: bfloat16 [2, 4096, 1024], P('replica', 'fsdp'), may hold values from -6 to 6
- segments: int32 [2, 4096], P('replica'), may hold values from 0 to 2, as said below
- cotangent: bfloat16 [2, 4096, 1024], P('replica', 'fsdp'), may hold values from -6 to 6
- norm_gain_one: bfloat16 [1024], P('fsdp'), may hold values from 0.5 to 1.5
- in_weight: bfloat16 [1024, 3328], P('fsdp'), may hold values from -0.1875 to 0.1875
- step_weight: bfloat16 [1024, 24], P('fsdp'), may hold values from -0.1875 to 0.1875
- qkv_weight: bfloat16 [1024, 768], P('fsdp'), may hold values from -0.1875 to 0.1875
- ssm_out_weight: bfloat16 [1536, 1024], P('fsdp'), may hold values from -0.01953125 to 0.01953125
- attn_out_weight: bfloat16 [512, 1024], P('fsdp'), may hold values from -6 to 6
- decay_log: float32 [24], replicated, may hold values from -9 to -1
- step_bias: float32 [24], replicated, may hold values from -4 to -1
- skip_gain: float32 [24], replicated, may hold values from 0.5 to 1.5
- norm_gain_two: bfloat16 [1024], P('fsdp'), may hold values from 0.5 to 1.5
- gate_weight: bfloat16 [1024, 2048], P('fsdp'), may hold values from -0.1875 to 0.1875
- up_weight: bfloat16 [1024, 2048], P('fsdp'), may hold values from -0.1875 to 0.1875
- down_weight: bfloat16 [2048, 1024], P('fsdp'), may hold values from -0.125 to 0.125
Outputs:
- output: bfloat16 [2, 4096, 1024], P('replica', 'fsdp')
- tokens_grad: bfloat16 [2, 4096, 1024], P('replica', 'fsdp')
- norm_gain_one_grad: float32 [1024], P('fsdp')
- in_weight_grad: float32 [1024, 3328], P('fsdp')
- step_weight_grad: float32 [1024, 24], P('fsdp')
- qkv_weight_grad: float32 [1024, 768], P('fsdp')
- ssm_out_weight_grad: float32 [1536, 1024], P('fsdp')
- attn_out_weight_grad: float32 [512, 1024], P('fsdp')
- decay_log_grad: float32 [24], replicated
- step_bias_grad: float32 [24], replicated
- skip_gain_grad: float32 [24], replicated
- norm_gain_two_grad: float32 [1024], P('fsdp')
- gate_weight_grad: float32 [1024, 2048], P('fsdp')
- up_weight_grad: float32 [1024, 2048], P('fsdp')
- down_weight_grad: float32 [2048, 1024], P('fsdp')
Inputs may be any that keep to these rules, and one draw needn't show every extreme that they name: `segments`: each sequence holds three documents: the middle one starts within the first 256 tokens and ends within the last 256 tokens; document numbers never fall along a sequence.
All inputs are finite; a program needn't handle non-finite values.
Results may differ from a plain program's by a relative error of at most 0.0095.
The roundings to bfloat16 on the way count: a program that leaves them out, or rounds other values in their place, can miss the bound.
Values may be sent and summed in bfloat16 or wider, within the bound.
No kernel may reach another device: no remote copies, remote signals or barrier semaphores. Data moves between devices by JAX's collectives and lax.ppermute only.
A program may use at most 192 MiB of HBM per device.

v0:
```python
from functools import partial

import jax
import jax.numpy as jnp
from jax import lax
from jax.sharding import PartitionSpec as P

SSM_HEADS = 24
HEAD = 64
STATE = 128
Q_HEADS = 8
KV_HEADS = 2


EPSILON = 1e-05
HIGHEST = lax.Precision.HIGHEST
NEGATIVE = -1e30
KEY_BLOCK = 512


def prefix(value, axis, combine, identity, reverse):
    size, here = (lax.axis_size(axis), lax.axis_index(axis))
    everything = jax.tree.map(lambda part: lax.all_gather(part, axis), value)
    start = jax.tree.map(
        lambda part, zero: jnp.broadcast_to(jnp.asarray(zero, part.dtype), part.shape),
        value,
        identity,
    )

    def lap(k, before):
        at = size - 1 - k if reverse else k
        reached = at > here if reverse else at < here
        new = combine(before, jax.tree.map(lambda part: part[at], everything))
        return jax.tree.map(lambda a, b: jnp.where(reached, a, b), new, before)

    return lax.fori_loop(0, size, lap, start)


def to_low(values):
    return values.astype(jnp.bfloat16)


def matmul(left, right):
    return jnp.dot(left, right, preferred_element_type=jnp.float32)


def matmul_tn(left, right):
    return lax.dot_general(
        left, right, (((0,), (0,)), ((), ())), preferred_element_type=jnp.float32
    )


def matmul_nt(left, right):
    return lax.dot_general(
        left, right, (((1,), (1,)), ((), ())), preferred_element_type=jnp.float32
    )


def norm_back(grad_normed, normed, inverse):
    return inverse * (grad_normed - normed * jnp.mean(grad_normed * normed, axis=-1, keepdims=True))


def chain(earlier, later):
    return (earlier[0] * later[0], later[1] + later[0][:, None, None] * earlier[1])


def decays(step_raw, decay_log, step_bias):
    step_size = jax.nn.softplus(step_raw + step_bias)
    cumulate = jnp.cumsum(-jnp.exp(decay_log)[None, :] * step_size, axis=0)
    return (step_size, cumulate)


def ssm_summary(inputs, b_rows, step_raw, decay_log, step_bias, segment, previous):
    step_size, cumulate = decays(step_raw, decay_log, step_bias)
    carried_on = (segment == previous).astype(jnp.float32)
    last_same = (segment == segment[-1]).astype(jnp.float32)[:, None]
    weight_tail = jnp.exp(cumulate[-1][None, :] - cumulate) * last_same * step_size
    fresh_state = jnp.einsum("sh,shp,sn->hpn", weight_tail, inputs, b_rows, precision=HIGHEST)
    keep_factor = jnp.exp(cumulate[-1]) * carried_on[-1]
    return (fresh_state, keep_factor)


def ssm_output(
    state_in,
    inputs,
    b_rows,
    c_rows,
    step_raw,
    decay_log,
    step_bias,
    skip_gain,
    gate_z,
    segment,
    previous,
):
    step_size, cumulate = decays(step_raw, decay_log, step_bias)
    positions = jnp.arange(segment.shape[0])
    allowed = (segment[:, None] == segment[None, :]) & (positions[:, None] >= positions[None, :])
    allowed_f = allowed.astype(jnp.float32)[:, :, None]
    within = (
        jnp.exp(jnp.where(allowed[:, :, None], cumulate[:, None, :] - cumulate[None, :, :], 0.0))
        * allowed_f
    )
    cross_cb = jnp.dot(c_rows, b_rows.T, precision=HIGHEST, preferred_element_type=jnp.float32)
    mixing = cross_cb[:, :, None] * within * step_size[None, :, :]
    direct = jnp.einsum("tsh,shp->thp", mixing, inputs, precision=HIGHEST)
    carried_on = (segment == previous).astype(jnp.float32)
    entry_gain = jnp.exp(cumulate) * carried_on[:, None]
    carried = (
        jnp.einsum("hpn,tn->thp", state_in, c_rows, precision=HIGHEST) * entry_gain[:, :, None]
    )
    return (direct + carried + skip_gain[None, :, None] * inputs) * jax.nn.silu(gate_z)


def block_scores(queries, q_place, q_seg, q_scale, key_block, k_place, k_seg):
    raw_scores = (
        jnp.einsum("kgtd,jkd->kgtj", queries, key_block, preferred_element_type=jnp.float32)
        * q_scale
    )
    allowed = (k_place[None, :] <= q_place[:, None]) & (k_seg[None, :] == q_seg[:, None])
    return jnp.where(allowed[None, None], raw_scores, NEGATIVE)


def on_device(
    tokens,
    segments,
    cotangent,
    norm_gain_one,
    in_weight,
    step_weight,
    qkv_weight,
    ssm_out_weight,
    attn_out_weight,
    decay_log,
    step_bias,
    skip_gain,
    norm_gain_two,
    gate_weight,
    up_weight,
    down_weight,
):
    tok_rows = tokens.shape[1]
    seq_len = tok_rows * lax.axis_size("fsdp")
    blocks = seq_len // KEY_BLOCK
    inner_width = SSM_HEADS * HEAD
    q_width = Q_HEADS * HEAD
    k_width = KV_HEADS * HEAD
    group_size = Q_HEADS // KV_HEADS
    q_scale = HEAD ** (-0.5)
    first_row = lax.axis_index("fsdp") * tok_rows
    seg_all = segments[0]
    seg_mine = lax.dynamic_slice_in_dim(seg_all, first_row, tok_rows)
    seg_before = jnp.where(
        first_row > 0,
        lax.dynamic_index_in_dim(seg_all, jnp.maximum(first_row - 1, 0), keepdims=False),
        -1,
    )
    q_place = first_row + jnp.arange(tok_rows, dtype=jnp.int32)
    key_place = jnp.arange(seq_len, dtype=jnp.int32).reshape(blocks, KEY_BLOCK)
    key_seg = seg_all.reshape(blocks, KEY_BLOCK)
    inputs = tokens[0].astype(jnp.float32)
    upstream = cotangent[0]
    gain_one, w_in, w_step, w_qkv, w_ssm_out, w_attn_out = (
        lax.all_gather(norm_gain_one, "fsdp", axis=0, tiled=True),
        lax.all_gather(in_weight, "fsdp", axis=0, tiled=True),
        lax.all_gather(step_weight, "fsdp", axis=0, tiled=True),
        lax.all_gather(qkv_weight, "fsdp", axis=0, tiled=True),
        lax.all_gather(ssm_out_weight, "fsdp", axis=0, tiled=True),
        lax.all_gather(attn_out_weight, "fsdp", axis=0, tiled=True),
    )
    inverse_one = lax.rsqrt(jnp.mean(inputs * inputs, axis=-1, keepdims=True) + EPSILON)
    normed_one = inputs * inverse_one
    h_one = to_low(normed_one * gain_one.astype(jnp.float32))
    ssm_in = matmul(h_one, w_in)
    step_raw = matmul(h_one, w_step)
    qkv_rows = matmul(h_one, w_qkv)
    gate_z = ssm_in[:, :inner_width].reshape(tok_rows, SSM_HEADS, HEAD)
    ssm_x = ssm_in[:, inner_width : 2 * inner_width].reshape(tok_rows, SSM_HEADS, HEAD)
    b_rows = ssm_in[:, 2 * inner_width : 2 * inner_width + STATE]
    c_rows = ssm_in[:, 2 * inner_width + STATE :]
    summary_fn = partial(ssm_summary, segment=seg_mine, previous=seg_before)
    (fresh_state, keep_factor), summary_back = jax.vjp(
        summary_fn, ssm_x, b_rows, step_raw, decay_log, step_bias
    )
    identity = (jnp.ones_like(keep_factor), jnp.zeros_like(fresh_state))
    incoming = prefix((keep_factor, fresh_state), "fsdp", chain, identity, False)
    state_in = incoming[1]
    output_fn = partial(ssm_output, segment=seg_mine, previous=seg_before)
    gated, output_back = jax.vjp(
        output_fn,
        state_in,
        ssm_x,
        b_rows,
        c_rows,
        step_raw,
        decay_log,
        step_bias,
        skip_gain,
        gate_z,
    )
    gated_low = to_low(gated.reshape(tok_rows, inner_width))
    queries = (
        to_low(qkv_rows[:, :q_width])
        .reshape(tok_rows, KV_HEADS, group_size, HEAD)
        .transpose(1, 2, 0, 3)
    )
    kv_all = lax.all_gather(to_low(qkv_rows[:, q_width:]), "fsdp", axis=0, tiled=True)
    key_rows = kv_all[:, :k_width].reshape(blocks, KEY_BLOCK, KV_HEADS, HEAD)
    value_rows = kv_all[:, k_width:].reshape(blocks, KEY_BLOCK, KV_HEADS, HEAD)
    score_fn = partial(block_scores, queries, q_place, seg_mine, q_scale)

    def running(carry_in, pieces):
        top_now, total_now = carry_in
        key_block, k_place, k_seg = pieces
        scores = score_fn(key_block, k_place, k_seg)
        top_new = jnp.maximum(top_now, jnp.max(scores, axis=-1))
        live = (scores > 0.5 * NEGATIVE).astype(jnp.float32)
        exps = jnp.exp(scores - top_new[..., None]) * live
        return ((top_new, total_now * jnp.exp(top_now - top_new) + jnp.sum(exps, axis=-1)), None)

    top_init = jnp.full((KV_HEADS, group_size, tok_rows), NEGATIVE, jnp.float32)
    (top_end, total_end), unused = lax.scan(
        running, (top_init, jnp.zeros_like(top_init)), (key_rows, key_place, key_seg)
    )
    log_total = top_end + jnp.log(total_end)

    def weighted(acc_out, pieces):
        key_block, value_block, k_place, k_seg = pieces
        weights_low = to_low(jnp.exp(score_fn(key_block, k_place, k_seg) - log_total[..., None]))
        return (
            acc_out
            + jnp.einsum(
                "kgtj,jkd->kgtd", weights_low, value_block, preferred_element_type=jnp.float32
            ),
            None,
        )

    attended, unused = lax.scan(
        weighted,
        jnp.zeros((KV_HEADS, group_size, tok_rows, HEAD), jnp.float32),
        (key_rows, value_rows, key_place, key_seg),
    )
    attended_low = to_low(attended.transpose(2, 0, 1, 3).reshape(tok_rows, q_width))
    resid = inputs + matmul(gated_low, w_ssm_out) + matmul(attended_low, w_attn_out)
    gain_two, w_gate, w_up, w_down = (
        lax.all_gather(norm_gain_two, "fsdp", axis=0, tiled=True),
        lax.all_gather(gate_weight, "fsdp", axis=0, tiled=True),
        lax.all_gather(up_weight, "fsdp", axis=0, tiled=True),
        lax.all_gather(down_weight, "fsdp", axis=0, tiled=True),
    )
    inverse_two = lax.rsqrt(jnp.mean(resid * resid, axis=-1, keepdims=True) + EPSILON)
    normed_two = resid * inverse_two
    h_two = to_low(normed_two * gain_two.astype(jnp.float32))
    gate_pre = matmul(h_two, w_gate)
    up_pre = matmul(h_two, w_up)
    activated = to_low(jax.nn.silu(gate_pre) * up_pre)
    result = resid + matmul(activated, w_down)
    d_act = matmul_nt(upstream, w_down)
    g_down = matmul_tn(activated, upstream)
    sigmoid_gate = jax.nn.sigmoid(gate_pre)
    d_gate = to_low(d_act * up_pre * sigmoid_gate * (1.0 + gate_pre * (1.0 - sigmoid_gate)))
    d_up = to_low(d_act * gate_pre * sigmoid_gate)
    g_gate = matmul_tn(h_two, d_gate)
    g_up = matmul_tn(h_two, d_up)
    d_h_two = matmul_nt(d_gate, w_gate) + matmul_nt(d_up, w_up)
    g_norm_two = jnp.sum(d_h_two * normed_two, axis=0)
    d_resid = upstream.astype(jnp.float32) + norm_back(
        d_h_two * gain_two.astype(jnp.float32), normed_two, inverse_two
    )
    mlp_grads = (
        lax.psum_scatter(g_norm_two, "fsdp", scatter_dimension=0, tiled=True),
        lax.psum_scatter(g_gate, "fsdp", scatter_dimension=0, tiled=True),
        lax.psum_scatter(g_up, "fsdp", scatter_dimension=0, tiled=True),
        lax.psum_scatter(g_down, "fsdp", scatter_dimension=0, tiled=True),
    )
    d_branch = to_low(d_resid)
    g_ssm_out = matmul_tn(gated_low, d_branch)
    g_attn_out = matmul_tn(attended_low, d_branch)
    d_gated = matmul_nt(d_branch, w_ssm_out)
    d_attended = to_low(matmul_nt(d_branch, w_attn_out))
    d_heads = d_attended.reshape(tok_rows, KV_HEADS, group_size, HEAD).transpose(1, 2, 0, 3)

    def spread(acc_sum, pieces):
        key_block, value_block, k_place, k_seg = pieces
        weights_now = jnp.exp(score_fn(key_block, k_place, k_seg) - log_total[..., None])
        d_weights = jnp.einsum(
            "kgtd,jkd->kgtj", d_heads, value_block, preferred_element_type=jnp.float32
        )
        return (acc_sum + jnp.sum(weights_now * d_weights, axis=-1), None)

    row_dot, unused = lax.scan(
        spread,
        jnp.zeros((KV_HEADS, group_size, tok_rows), jnp.float32),
        (key_rows, value_rows, key_place, key_seg),
    )

    def query_grad(acc_query, pieces):
        key_block, value_block, k_place, k_seg = pieces
        weights_now = jnp.exp(score_fn(key_block, k_place, k_seg) - log_total[..., None])
        d_weights = jnp.einsum(
            "kgtd,jkd->kgtj", d_heads, value_block, preferred_element_type=jnp.float32
        )
        d_scores = to_low(weights_now * (d_weights - row_dot[..., None]))
        return (
            acc_query
            + jnp.einsum("kgtj,jkd->kgtd", d_scores, key_block, preferred_element_type=jnp.float32),
            None,
        )

    d_query, unused = lax.scan(
        query_grad,
        jnp.zeros((KV_HEADS, group_size, tok_rows, HEAD), jnp.float32),
        (key_rows, value_rows, key_place, key_seg),
    )
    d_query_low = to_low((d_query * q_scale).transpose(2, 0, 1, 3).reshape(tok_rows, q_width))
    sub_rows = KEY_BLOCK

    def piece_term(begin_row):
        kv_block = lax.dynamic_slice_in_dim(kv_all, begin_row, sub_rows, 0)
        key_block = kv_block[:, :k_width].reshape(sub_rows, KV_HEADS, HEAD)
        value_block = kv_block[:, k_width:].reshape(sub_rows, KV_HEADS, HEAD)
        k_place = begin_row + jnp.arange(sub_rows, dtype=jnp.int32)
        k_seg = lax.dynamic_slice_in_dim(seg_all, begin_row, sub_rows)
        weights_now = jnp.exp(score_fn(key_block, k_place, k_seg) - log_total[..., None])
        d_weights = jnp.einsum(
            "kgtd,jkd->kgtj", d_heads, value_block, preferred_element_type=jnp.float32
        )
        d_scores = to_low(weights_now * (d_weights - row_dot[..., None]))
        d_keys = (
            jnp.einsum("kgtj,kgtd->jkd", d_scores, queries, preferred_element_type=jnp.float32)
            * q_scale
        )
        d_values = jnp.einsum(
            "kgtj,kgtd->jkd", to_low(weights_now), d_heads, preferred_element_type=jnp.float32
        )
        return jnp.concatenate(
            [d_keys.reshape(sub_rows, k_width), d_values.reshape(sub_rows, k_width)], axis=1
        )

    begin_rows = sub_rows * jnp.arange(
        lax.axis_size("fsdp") * tok_rows // sub_rows, dtype=jnp.int32
    )
    d_kv = lax.psum_scatter(
        lax.map(piece_term, begin_rows).reshape(lax.axis_size("fsdp") * tok_rows, 2 * k_width),
        "fsdp",
        scatter_dimension=0,
        tiled=True,
    )
    d_qkv = jnp.concatenate([d_query_low, to_low(d_kv)], axis=1)
    grads_y = output_back(d_gated.reshape(tok_rows, SSM_HEADS, HEAD))
    later_grad = prefix((keep_factor, grads_y[0]), "fsdp", chain, identity, True)[1]
    grads_s = summary_back((later_grad, jnp.sum(later_grad * state_in, axis=(1, 2))))
    d_gate_z = grads_y[8].reshape(tok_rows, inner_width)
    d_ssm_x = (grads_y[1] + grads_s[0]).reshape(tok_rows, inner_width)
    d_b_rows = grads_y[2] + grads_s[1]
    d_c_rows = grads_y[3]
    d_step_low = to_low(grads_y[4] + grads_s[2])
    g_decay = grads_y[5] + grads_s[3]
    g_bias = grads_y[6] + grads_s[4]
    g_skip = grads_y[7]
    d_ssm_low = to_low(jnp.concatenate([d_gate_z, d_ssm_x, d_b_rows, d_c_rows], axis=1))
    g_in = matmul_tn(h_one, d_ssm_low)
    g_step = matmul_tn(h_one, d_step_low)
    g_qkv = matmul_tn(h_one, d_qkv)
    d_h_one = matmul_nt(d_ssm_low, w_in) + matmul_nt(d_step_low, w_step) + matmul_nt(d_qkv, w_qkv)
    g_norm_one = jnp.sum(d_h_one * normed_one, axis=0)
    d_inputs = d_resid + norm_back(d_h_one * gain_one.astype(jnp.float32), normed_one, inverse_one)
    mixer_grads = (
        lax.psum_scatter(g_norm_one, "fsdp", scatter_dimension=0, tiled=True),
        lax.psum_scatter(g_in, "fsdp", scatter_dimension=0, tiled=True),
        lax.psum_scatter(g_step, "fsdp", scatter_dimension=0, tiled=True),
        lax.psum_scatter(g_qkv, "fsdp", scatter_dimension=0, tiled=True),
        lax.psum_scatter(g_ssm_out, "fsdp", scatter_dimension=0, tiled=True),
        lax.psum_scatter(g_attn_out, "fsdp", scatter_dimension=0, tiled=True),
    )
    summed = lax.psum(
        (
            mixer_grads[0],
            mixer_grads[1],
            mixer_grads[2],
            mixer_grads[3],
            mixer_grads[4],
            mixer_grads[5],
            mlp_grads[0],
            mlp_grads[1],
            mlp_grads[2],
            mlp_grads[3],
        ),
        "replica",
    )
    head_grads = lax.psum((g_decay, g_bias, g_skip), ("replica", "fsdp"))
    outs_gain_one = summed[0]
    outs_gain_two = summed[6]
    matrices = (
        summed[1],
        summed[2],
        summed[3],
        summed[4],
        summed[5],
        summed[7],
        summed[8],
        summed[9],
    )
    return (
        to_low(result)[None],
        to_low(d_inputs)[None],
        outs_gain_one,
        matrices[0],
        matrices[1],
        matrices[2],
        matrices[3],
        matrices[4],
        head_grads[0],
        head_grads[1],
        head_grads[2],
        outs_gain_two,
        matrices[5],
        matrices[6],
        matrices[7],
    )


def solution(mesh):
    return jax.shard_map(
        on_device,
        mesh=mesh,
        in_specs=(
            P("replica", "fsdp", None),
            P("replica", None),
            P("replica", "fsdp", None),
            P("fsdp"),
            P("fsdp", None),
            P("fsdp", None),
            P("fsdp", None),
            P("fsdp", None),
            P("fsdp", None),
            P(),
            P(),
            P(),
            P("fsdp"),
            P("fsdp", None),
            P("fsdp", None),
            P("fsdp", None),
        ),
        out_specs=(
            P("replica", "fsdp", None),
            P("replica", "fsdp", None),
            P("fsdp"),
            P("fsdp", None),
            P("fsdp", None),
            P("fsdp", None),
            P("fsdp", None),
            P("fsdp", None),
            P(),
            P(),
            P(),
            P("fsdp"),
            P("fsdp", None),
            P("fsdp", None),
            P("fsdp", None),
        ),
        check_vma=False,
    )
```

profile of v0, /device:TPU:0, one launch (start us, length us, event | category | flops | bytes accessed | tf_op | source)
XLA Modules:
  0.0 1713.1 jit_solution(2332871724228074795)
XLA Ops:
  12.4 35.2 %all-reduce.10 = (bf16[1024]{0:T(1024)(128)(2,1)S(1)}, bf16[1024]{0:T(1024)(128)(2,1)S(1)}) all-reduce(bf16[1024]{0:T(1024)(128)(2,1)S(1)} %dynamic-update-slice, bf16[1024]{0:T(1024)(128)(2,1)S(1)} %dynamic-update-slice.1), channel_id=1, replica_groups=mesh['replica'=2,'fsdp'=16] {'fsdp'}, use_global_device_ids=true, to_apply=%add.2 | all-reduce | flops 2048 | bytes 8192
  58.3 19.8 %all-gather.2 = bf16[16,64,24]{1,2,0:T(8,128)(2,1)S(1)} all-gather(bf16[1,64,24]{1,2,0:T(8,128)(2,1)S(1)} %bitcast.610), channel_id=1, replica_groups=mesh['replica'=2,'fsdp'=16] {'fsdp'}, dimensions={0}, use_global_device_ids=true | all-gather | bytes 52224 | tf_op jit(solution)/shard_map/all_gather | solution.py:166
  81.1 38.2 %all-gather.15.cloned.1.call-done = bf16[1024,3328]{1,0:T(8,128)(2,1)} async-done(((bf16[64,3328]{1,0:T(8,128)(2,1)}), bf16[1024,3328]{1,0:T(8,128)(2,1)}) %all-gather.15.cloned.1.call-update) | async-done | bytes 6815760 | tf_op jit(solution)/shard_map/all_gather | solution.py:165
  138.4 20.1 %all-gather.3 = f32[16,1,24]{2,1,0:T(1,128)} all-gather(f32[1,1,24]{2,1,0:T(1,128)S(1)} %bitcast.612), channel_id=1, replica_groups=mesh['replica'=2,'fsdp'=16] {'fsdp'}, dimensions={0}, use_global_device_ids=true | all-gather | bytes 1632 | tf_op jit(solution)/shard_map/all_gather | solution.py:23
  172.6 59.9 %while.89 = (s32[]{:T(128)}, f32[2,4,256]{2,1,0:T(4,128)S(1)}, f32[2,4,256]{2,1,0:T(4,128)S(1)}, s32[8,512]{1,0:T(8,128)S(1)}, s32[8,512]{1,0:T(8,128)S(1)}, /*i...) while((s32[]{:T(128)}, f32[2,4,256]{2,1,0:T(4,128)S(1)}, ...), condition=%wide.region_8.10_spmd.clone, body=%wide.region_5.9_spmd.clone.sunk | while | flops 144058624 | bytes 9297536 | solution.py:222
  243.5 22.6 %while.90 = (s32[]{:T(128)}, f32[2,4,256,64]{2,3,1,0:T(8,128)S(1)}, s32[8,512]{1,0:T(8,128)S(1)}, s32[8,512]{1,0:T(8,128)S(1)}, s32[256]{0:T(256)S(1)}, /*index=...) while((s32[]{:T(128)}, f32[2,4,256,64]{2,3,1,0:T(8,128)S(1)}, ...), condition=%wide.region_10.12_spmd.clone, body=%wide.region_9.11_spmd.clone.sunk | while | flops 273285376 | bytes 1859719 | solution.py:238
  272.5 32.1 %while.88 = (s32[]{:T(128)}, f32[24,64,128]{2,1,0:T(8,128)S(1)}, s32[]{:T(128)}, f32[16,24,64,128]{3,2,1,0:T(8,128)}, f32[16,24]{1,0:T(8,128)}, /*index=5*/s32[]{:T(128)}, s32[]{:T(128)}) while((s32[]{:T(128)}, f32[24,64,128]{2,1,0:T(8,128)S(1)}, s32[]{:T(128)}, f32[16,24,64,128]{3,2,1,0:T(8,128)}, f32[16,24]{1,0:T(8,128)}, ...), condition=%wide.region_4.6_spmd.clone, body=%wide.region_3.5_spmd.clone.sunk | while | flops 786436 | bytes 2359689 | solution.py:36
  308.0 10.9 multiply_convert_fusion.3
  323.2 25.5 %all-gather.23.cloned.1.call-done = bf16[512,1024]{1,0:T(8,128)(2,1)} async-done(((bf16[32,1024]{1,0:T(8,128)(2,1)}), bf16[512,1024]{1,0:T(8,128)(2,1)}) %all-gather.23.cloned.1.call-update) | async-done | bytes 1048592 | tf_op jit(solution)/shard_map/all_gather | solution.py:169
  350.9 49.4 %all-gather.25.cloned.1.call-done = bf16[1024,2048]{1,0:T(8,128)(2,1)} async-done(((bf16[64,2048]{1,0:T(8,128)(2,1)}), bf16[1024,2048]{1,0:T(8,128)(2,1)}) %all-gather.25.cloned.1.call-update) | async-done | bytes 4194320 | tf_op jit(solution)/shard_map/all_gather | solution.py:247
  405.1 46.4 %all-gather.27.cloned.1.call-done = bf16[1024,2048]{1,0:T(8,128)(2,1)} async-done(((bf16[64,2048]{1,0:T(8,128)(2,1)}), bf16[1024,2048]{1,0:T(8,128)(2,1)}) %all-gather.27.cloned.1.call-update) | async-done | bytes 4194320 | tf_op jit(solution)/shard_map/all_gather | solution.py:248
  456.4 46.4 %all-gather.29.cloned.1.call-done = bf16[2048,1024]{1,0:T(8,128)(2,1)} async-done(((bf16[128,1024]{1,0:T(8,128)(2,1)}), bf16[2048,1024]{1,0:T(8,128)(2,1)}) %all-gather.29.cloned.1.call-update) | async-done | bytes 4194320 | tf_op jit(solution)/shard_map/all_gather | solution.py:249
  502.8 6.6 multiply_convert_fusion
  517.9 34.5 %while.92 = (s32[]{:T(128)}, f32[2,4,256]{2,1,0:T(4,128)S(1)}, s32[8,512]{1,0:T(8,128)S(1)}, s32[8,512]{1,0:T(8,128)S(1)}, s32[256]{0:T(256)S(1)}, /*index=5*/bf...) while((s32[]{:T(128)}, f32[2,4,256]{2,1,0:T(4,128)S(1)}, ...), condition=%wide.region_28.30_spmd.clone, body=%wide.region_26.29_spmd.clone.sunk | while | flops 274073856 | bytes 9494671 | solution.py:291
  552.4 128.8 %while.87 = (s32[]{:T(128)}, f32[8,512,256]{2,1,0:T(8,128)}, s32[8]{0:T(128)S(1)}, s32[4096]{0:T(1024)S(1)}, s32[256]{0:T(256)S(1)}, /*index=5*/bf16[4096,256]{1...) while((s32[]{:T(128)}, f32[8,512,256]{2,1,0:T(8,128)}, ...), condition=%wide.region_32.34_spmd.clone, body=%wide.region_31.33_spmd.clone.sunk | while | flops 547947264 | bytes 19044060 | solution.py:344
  707.9 71.0 %while.93 = (s32[]{:T(128)}, f32[2,4,256,64]{2,3,1,0:T(8,128)}, s32[8,512]{1,0:T(8,128)S(1)}, s32[8,512]{1,0:T(8,128)S(1)}, s32[256]{0:T(256)S(1)}, /*index=5*/b...) while((s32[]{:T(128)}, f32[2,4,256,64]{2,3,1,0:T(8,128)}, ...), condition=%wide.region_30.32_spmd.clone, body=%wide.region_29.31_spmd.clone.sunk | while | flops 409600256 | bytes 10650263 | solution.py:310
  796.6 6.1 fusion.151
  806.4 12.8 fusion.85
  821.2 33.5 %all-gather.33.cloned.1.call-done = f32[384,64,128]{2,1,0:T(8,128)} async-done(((f32[24,64,128]{2,1,0:T(8,128)}), f32[384,64,128]{2,1,0:T(8,128)}) %all-gather.33.cloned.1.call-update) | async-done | bytes 12582928 | tf_op jit(solution)/shard_map/all_gather | solution.py:23
  854.7 32.5 %while.91 = (s32[]{:T(128)}, f32[24,64,128]{2,1,0:T(8,128)S(1)}, s32[]{:T(128)}, f32[16,24,64,128]{3,2,1,0:T(8,128)}, f32[16,24]{1,0:T(8,128)}, /*index=5*/s32[]{:T(128)}, s32[]{:T(128)}, s32[]{:T(128)}, s32[]{:T(128)}) while((s32[]{:T(128)}, f32[24,64,128]{2,1,0:T(8,128)S(1)}, s32[]{:T(128)}, f32[16,24,64,128]{3,2,1,0:T(8,128)}, ...), condition=%wide.region_14.16_spmd.clone, body=%wide.region_13.15_spmd.clone.sunk | while | flops 786440 | bytes 2359751 | solution.py:36
  894.2 6.2 fusion.104
  901.3 7.0 fusion.155
  920.4 86.3 %reduce-scatter.18.cloned.1.call-done = f32[96,1024]{1,0:T(8,128)} async-done(((f32[1536,1024]{1,0:T(8,128)}), f32[96,1024]{1,0:T(8,128)}) %reduce-scatter.18.cloned.1.call-update) | async-done | bytes 393232 | tf_op jit(solution)/shard_map/reduce_scatter | solution.py:373
  1006.7 69.6 %reduce-scatter.16.cloned.1.call-done = f32[64,768]{1,0:T(8,128)} async-done(((f32[1024,768]{1,0:T(8,128)}), f32[64,768]{1,0:T(8,128)}) %reduce-scatter.16.cloned.1.call-update) | async-done | bytes 196624 | tf_op jit(solution)/shard_map/reduce_scatter | solution.py:372
  1076.4 108.1 %reduce-scatter.22.cloned.1.call-done = f32[64,2048]{1,0:T(8,128)} async-done(((f32[1024,2048]{1,0:T(8,128)}), f32[64,2048]{1,0:T(8,128)}) %reduce-scatter.22.cloned.1.call-update) | async-done | bytes 524304 | tf_op jit(solution)/shard_map/reduce_scatter | solution.py:272
  1184.4 108.9 %reduce-scatter.24.cloned.1.call-done = f32[64,2048]{1,0:T(8,128)} async-done(((f32[1024,2048]{1,0:T(8,128)}), f32[64,2048]{1,0:T(8,128)}) %reduce-scatter.24.cloned.1.call-update) | async-done | bytes 524304 | tf_op jit(solution)/shard_map/reduce_scatter | solution.py:273
  1293.3 108.9 %reduce-scatter.26.cloned.1.call-done = f32[128,1024]{1,0:T(8,128)} async-done(((f32[2048,1024]{1,0:T(8,128)}), f32[128,1024]{1,0:T(8,128)}) %reduce-scatter.26.cloned.1.call-update) | async-done | bytes 524304 | tf_op jit(solution)/shard_map/reduce_scatter | solution.py:274
  1402.1 146.3 %reduce-scatter.14.cloned.1.call-done = f32[64,3328]{1,0:T(8,128)} async-done(((f32[1024,3328]{1,0:T(8,128)}), f32[64,3328]{1,0:T(8,128)}) %reduce-scatter.14.cloned.1.call-update) | async-done | bytes 851984 | tf_op jit(solution)/shard_map/reduce_scatter | solution.py:370
  1554.0 39.4 %all-reduce.6 = (f32[24]{0:T(128)}, f32[24]{0:T(128)}, f32[24]{0:T(128)}) all-reduce(f32[24]{0:T(128)S(1)} %add_multiply_fusion, f32[24]{0:T(128)S(1)} %add.295, f32[24]{0:T(128)S(1)} %reduce_sum.252), channel_id=1, replica_groups=mesh['replica'=2,'fsdp'=16] {'replica','fsdp'}, use_global_device_ids=true, to_apply=%region_50.52 | all-reduce | flops 72 | bytes 576 | tf_op jit(solution)/shard_map/psum | solution.py:391
  1600.7 31.9 %all-reduce.7 = (f32[1024]{0:T(1024)S(1)}, f32[1024]{0:T(1024)S(1)}) all-reduce(f32[1024]{0:T(1024)S(1)} %get-tuple-element.958, f32[1024]{0:T(1024)S(1)} %copy-done.66), channel_id=5, replica_groups=mesh['replica'=2,'fsdp'=16] {'fsdp'}, use_global_device_ids=true, to_apply=%region_36.38.clone | all-reduce | flops 2048 | bytes 16384
  1636.4 9.0 all-reduce.8
  1645.4 50.9 %all-reduce.13.cloned.1.call-done = (f32[64,3328]{1,0:T(8,128)}, f32[64,768]{1,0:T(8,128)}, f32[96,1024]{1,0:T(8,128)}, f32[32,1024]{1,0:T(8,128)}, f32[64,2048]...) async-done(((f32[64,3328]{1,0:T(8,128)}, f32[64,768]{1,0:T(8,128)}, f32[96,1024]{1,0:T(8,128)}, f32[32,1024]{1,0:T(8,128)}, f32[64,2048]{1,0:T(8,128)}, ...) | async-done | bytes 3145744 | tf_op jit(solution)/shard_map/psum | solution.py:376
  (705 shorter events, 553.1 us)
Async XLA Ops:
  7.2 71.2 %copy-start.4 = (bf16[1,256,1024]{2,1,0:T(8,128)(2,1)S(1)}, bf16[1,256,1024]{2,1,0:T(8,128)(2,1)}, u32[]{:S(2)}) copy-start(bf16[1,256,1024]{2,1,0:T(8,128)(2,1)} %param.31) | copy-start | bytes 1572868
  7.2 71.1 %copy-start.78 = (f32[24]{0:T(128)S(1)}, f32[24]{0:T(128)}, u32[]{:S(2)}) copy-start(f32[24]{0:T(128)} %param.40) | copy-start | bytes 292
  7.2 71.1 %copy-start.82 = (f32[24]{0:T(128)S(1)}, f32[24]{0:T(128)}, u32[]{:S(2)}) copy-start(f32[24]{0:T(128)} %param.41) | copy-start | bytes 292
  7.2 45.5 %all-gather.19.cloned.1.call-start = ((), (), s32[]{:S(2)}) async-start(), calls=%async_computation.11 | async-start | bytes 1671168 | tf_op jit(solution)/shard_map/all_gather | solution.py:167
  8.0 111.3 %all-gather.15.cloned.1.call-start = ((), (), s32[]{:S(2)}) async-start(), calls=%async_computation.9 | async-start | bytes 7241728 | tf_op jit(solution)/shard_map/all_gather | solution.py:165
  8.7 153.3 %all-gather.21.cloned.1.call-start = ((), (), s32[]{:S(2)}) async-start(), calls=%async_computation.12 | async-start | bytes 2228224 | tf_op jit(solution)/shard_map/all_gather | solution.py:207
  48.9 75.4 %copy-start.55 = (f32[256]{0:T(256)}, f32[256]{0:T(256)S(1)}, u32[]{:S(2)}) copy-start(f32[256]{0:T(256)S(1)} %add_rsqrt_fusion.1) | copy-start | bytes 3076
  55.7 216.7 %all-gather.31.cloned.1.call-start = ((), (), s32[]{:S(2)}) async-start(), calls=%async_computation.25 | async-start | bytes 13369344 | tf_op jit(solution)/shard_map/all_gather | solution.py:23
  79.6 227.2 %copy-start.50 = (f32[256,24]{0,1:T(8,128)}, f32[256,24]{0,1:T(8,128)S(1)}, u32[]{:S(2)}) copy-start(f32[256,24]{0,1:T(8,128)S(1)} %bitcast_bitcast_fusion.2) | copy-start | bytes 73732
  81.1 615.7 %copy-start.45 = (f32[256,24]{0,1:T(8,128)}, f32[256,24]{0,1:T(8,128)S(1)}, u32[]{:S(2)}) copy-start(f32[256,24]{0,1:T(8,128)S(1)} %get-tuple-element.1139) | copy-start | bytes 73732
  132.3 186.7 %all-gather.17.cloned.1.call-start = ((), (), s32[]{:S(2)}) async-start(), calls=%async_computation.10 | async-start | bytes 3342336 | tf_op jit(solution)/shard_map/all_gather | solution.py:168
  132.9 215.8 %all-gather.23.cloned.1.call-start = ((), (), s32[]{:S(2)}) async-start(), calls=%async_computation.13 | async-start | bytes 1114112 | tf_op jit(solution)/shard_map/all_gather | solution.py:169
  133.5 266.9 %all-gather.25.cloned.1.call-start = ((), (), s32[]{:S(2)}) async-start(), calls=%async_computation.14 | async-start | bytes 4456448 | tf_op jit(solution)/shard_map/all_gather | solution.py:247
  134.2 317.4 %all-gather.27.cloned.1.call-start = ((), (), s32[]{:S(2)}) async-start(), calls=%async_computation.15 | async-start | bytes 4456448 | tf_op jit(solution)/shard_map/all_gather | solution.py:248
  135.0 367.9 %all-gather.29.cloned.1.call-start = ((), (), s32[]{:S(2)}) async-start(), calls=%async_computation.16 | async-start | bytes 4456448 | tf_op jit(solution)/shard_map/all_gather | solution.py:249
  135.7 644.4 %reduce-scatter.12.cloned.1.call-start = ((), (), s32[]{:S(2)}) async-start(), calls=%async_computation.17 | async-start | bytes 4456448 | tf_op jit(solution)/shard_map/reduce_scatter | solution.py:343
  350.9 100.6 %copy-start.11 = (bf16[256,1024]{1,0:T(8,128)(2,1)}, bf16[256,1024]{1,0:T(8,128)(2,1)S(1)}, u32[]{:S(2)}) copy-start(bf16[256,1024]{1,0:T(8,128)(2,1)S(1)} %multiply_convert_fusion.4) | copy-start | bytes 1572868
  405.1 97.7 %copy-start.13 = (bf16[1,256,1024]{2,1,0:T(8,128)(2,1)S(1)}, bf16[1,256,1024]{2,1,0:T(8,128)(2,1)}, u32[]{:S(2)}) copy-start(bf16[1,256,1024]{2,1,0:T(8,128)(2,1)} %param.33) | copy-start | bytes 1572868
  681.2 173.5 %all-gather.33.cloned.1.call-start = ((), (), s32[]{:S(2)}) async-start(), calls=%async_computation.26 | async-start | bytes 13369344 | tf_op jit(solution)/shard_map/all_gather | solution.py:23
  701.2 219.2 %reduce-scatter.20.cloned.1.call-start = ((), (), s32[]{:S(2)}) async-start(), calls=%async_computation.21 | async-start | bytes 2228224 | tf_op jit(solution)/shard_map/reduce_scatter | solution.py:374
  703.1 303.7 %reduce-scatter.18.cloned.1.call-start = ((), (), s32[]{:S(2)}) async-start(), calls=%async_computation.20 | async-start | bytes 6684672 | tf_op jit(solution)/shard_map/reduce_scatter | solution.py:373
  707.9 368.5 %reduce-scatter.16.cloned.1.call-start = ((), (), s32[]{:S(2)}) async-start(), calls=%async_computation.19 | async-start | bytes 3342336 | tf_op jit(solution)/shard_map/reduce_scatter | solution.py:372
  707.9 73.3 %copy-start.5 = (bf16[1,256,1024]{2,1,0:T(8,128)(2,1)S(1)}, bf16[1,256,1024]{2,1,0:T(8,128)(2,1)}, u32[]{:S(2)}) copy-start(bf16[1,256,1024]{2,1,0:T(8,128)(2,1)} %param.31) | copy-start | bytes 1572868
  707.9 73.3 %copy-start.56 = (f32[256]{0:T(256)S(1)}, f32[256]{0:T(256)}, u32[]{:S(2)}) copy-start(f32[256]{0:T(256)} %copy-done.55) | copy-start | bytes 3076
  783.7 400.8 %reduce-scatter.22.cloned.1.call-start = ((), (), s32[]{:S(2)}) async-start(), calls=%async_computation.22 | async-start | bytes 8912896 | tf_op jit(solution)/shard_map/reduce_scatter | solution.py:272
  789.5 503.8 %reduce-scatter.24.cloned.1.call-start = ((), (), s32[]{:S(2)}) async-start(), calls=%async_computation.23 | async-start | bytes 8912896 | tf_op jit(solution)/shard_map/reduce_scatter | solution.py:273
  795.5 606.7 %reduce-scatter.26.cloned.1.call-start = ((), (), s32[]{:S(2)}) async-start(), calls=%async_computation.24 | async-start | bytes 8912896 | tf_op jit(solution)/shard_map/reduce_scatter | solution.py:274
  802.8 745.7 %reduce-scatter.14.cloned.1.call-start = ((), (), s32[]{:S(2)}) async-start(), calls=%async_computation.18 | async-start | bytes 14483456 | tf_op jit(solution)/shard_map/reduce_scatter | solution.py:370
  908.5 727.2 %reduce-scatter.28.cloned.1.call-start = ((), (), s32[]{:S(2)}) async-start(), calls=%async_computation.27 | async-start | bytes 557056
  913.5 635.6 %copy-start.75 = (f32[1536]{0:T(1024)S(1)}, f32[1536]{0:T(1024)}, u32[]{:S(2)}) copy-start(f32[1536]{0:T(1024)} %get-tuple-element.1158) | copy-start | bytes 18436
  913.5 635.8 %copy-start.79 = (f32[24]{0:T(128)S(1)}, f32[24]{0:T(128)}, u32[]{:S(2)}) copy-start(f32[24]{0:T(128)} %param.40) | copy-start | bytes 292
  920.3 775.9 %all-reduce.13.cloned.1.call-start = ((), (), s32[]{:S(2)}) async-start(), calls=%async_computation.28 | async-start | bytes 6291456 | tf_op jit(solution)/shard_map/psum | solution.py:376
  (74 other events, 1233.5 us)
Sparse Core Ops, SparseCore 0:
  10.4 42.3 all-gather.18
  55.1 64.1 all-gather.14
  122.0 39.9 all-gather.20
  164.7 99.5 all-gather.30
  266.4 43.3 all-gather.16
  311.9 36.7 all-gather.22
  350.8 49.4 all-gather.24
  402.5 49.0 all-gather.26
  453.7 49.0 all-gather.28
  681.4 70.9 reduce-scatter.11
  754.9 99.7 all-gather.32
  858.7 59.7 reduce-scatter.19
  922.5 84.2 reduce-scatter.17
  1010.9 65.4 reduce-scatter.15
  1080.8 103.5 reduce-scatter.21
  1188.9 104.3 reduce-scatter.23
  1297.7 104.3 reduce-scatter.25
  1406.6 141.7 reduce-scatter.13
  1552.5 54.8 reduce-scatter.27
  1610.1 86.0 all-reduce.12
where the time goes:
time: 1720 us; the launch traced here: 1710 us
  waiting for transfers between devices  929 us (54%)
  matrix products  371 us (22%)
  blocking collectives  155 us (9%)
  other arithmetic  111 us (6%)
  local copies, waits for them, and re-layouts  109 us (6%)
  loops' own time  18.7 us (1%)
  between operations  18 us (1%)
    reduce_scatter x1, waiting for transfers between devices, on_device(): lax.psum_scatter(g_in, 'fsdp', scatter_dimension=0, tiled=True)  146 us
    reduce_scatter x1, waiting for transfers between devices, on_device(): lax.psum_scatter(g_up, 'fsdp', scatter_dimension=0, tiled=True)  109 us
    reduce_scatter x1, waiting for transfers between devices, on_device(): lax.psum_scatter(g_down, 'fsdp', scatter_dimension=0, tiled=True)  109 us
    reduce_scatter x1, waiting for transfers between devices, on_device(): lax.psum_scatter(g_gate, 'fsdp', scatter_dimension=0, tiled=True)  108 us
    dot_general x32, matrix products, block_scores(): jnp.einsum('kgtd,jkd->kgtj', queries, key_block, preferred_element_type=j...  93.6 us
    reduce_scatter x1, waiting for transfers between devices, on_device(): lax.psum_scatter(g_ssm_out, 'fsdp', scatter_dimension=0, tiled=True)  86.3 us
    reduce_scatter x1, waiting for transfers between devices, on_device(): lax.psum_scatter(g_qkv, 'fsdp', scatter_dimension=0, tiled=True)  69.6 us
    unnamed x2, blocking collectives  67.1 us
  transfers between devices with their start and end apart: 20, of which 15 were waited for; matrix products, arithmetic and copies ran while one was open for 24% of the time, Pallas kernels for 0%

commit v1 on v0

v1 whole, which is shorter than its diff:
```python
from functools import partial

import jax
import jax.numpy as jnp
from jax import lax
from jax.experimental import pallas as pl
from jax.experimental.pallas import tpu as pltpu
from jax.sharding import PartitionSpec as P

SSM_HEADS = 24
HEAD = 64
STATE = 128
Q_HEADS = 8
KV_HEADS = 2
SPLIT = 2
HEADS_HERE = SSM_HEADS // SPLIT
GROUP = Q_HEADS // KV_HEADS
INNER = HEADS_HERE * HEAD
EXTRA = 128

EPSILON = 1e-05
HIGHEST = lax.Precision.HIGHEST
NEGATIVE = -1e30
AXIS = "fsdp"


def to_low(values):
    return values.astype(jnp.bfloat16)


def matmul(left, right):
    return jnp.dot(left, right, preferred_element_type=jnp.float32)


def matmul_tn(left, right):
    return lax.dot_general(
        left, right, (((0,), (0,)), ((), ())), preferred_element_type=jnp.float32
    )


def matmul_nt(left, right):
    return lax.dot_general(
        left, right, (((1,), (1,)), ((), ())), preferred_element_type=jnp.float32
    )


def norm_back(grad_normed, normed, inverse):
    return inverse * (grad_normed - normed * jnp.mean(grad_normed * normed, axis=-1, keepdims=True))


def ring_order(chips):
    if chips % 4:
        return list(range(chips))
    wide = 2 if chips == 8 else 4
    if chips % wide:
        return list(range(chips))
    tall = chips // wide
    walk = [row * wide for row in range(tall)]
    for step, row in enumerate(reversed(range(tall))):
        columns = list(range(1, wide))
        if step % 2:
            columns.reverse()
        walk += [row * wide + column for column in columns]
    return walk


class Ring:
    def __init__(self, devices):
        self.chips = devices // SPLIT
        self.walk = ring_order(self.chips)
        place = [0] * self.chips
        for position, chip in enumerate(self.walk):
            place[chip] = position
        index = lax.axis_index(AXIS)
        self.core = lax.rem(index, SPLIT)
        self.chip = index // SPLIT
        self.walk_table = jnp.asarray(self.walk, jnp.int32)
        self.position = jnp.asarray(place, jnp.int32)[self.chip]
        ahead = []
        for position in range(self.chips):
            here, there = self.walk[position], self.walk[(position + 1) % self.chips]
            ahead += [(here * SPLIT + core, there * SPLIT + core) for core in range(SPLIT)]
        self.ahead = ahead
        self.back = [(there, here) for here, there in ahead]
        self.pair = [(device, device ^ 1) for device in range(devices)]

    def swap(self, value):
        return lax.ppermute(value, AXIS, self.pair)

    def chip_at(self, offset):
        return self.walk_table[lax.rem(self.position + offset + 2 * self.chips, self.chips)]

    def gather(self, block):
        chips = self.chips
        half = block.shape[-1] // 2
        everything = jnp.zeros((chips,) + block.shape, block.dtype)
        zeros = (0,) * block.ndim

        def put(whole, part, offset, start=0):
            return lax.dynamic_update_slice(
                whole, part[None], (self.chip_at(offset),) + zeros[:-1] + (start,)
            )

        everything = put(everything, block, 0)
        onward, backward = block, block
        for step in range(1, chips // 2):
            onward = lax.ppermute(onward, AXIS, self.ahead)
            backward = lax.ppermute(backward, AXIS, self.back)
            everything = put(everything, onward, -step)
            everything = put(everything, backward, step)
        onward = lax.ppermute(onward[..., :half], AXIS, self.ahead)
        backward = lax.ppermute(backward[..., half:], AXIS, self.back)
        everything = put(everything, onward, -(chips // 2))
        return put(everything, backward, chips // 2, half)

    def scatter(self, chunk_of, wire):
        chips = self.chips
        far = chunk_of(self.chip_at(chips // 2))
        half = far.shape[-1] // 2
        onward = lax.ppermute(far[..., :half].astype(wire), AXIS, self.ahead)
        backward = lax.ppermute(far[..., half:].astype(wire), AXIS, self.back)
        for step in range(chips // 2 - 1, 0, -1):
            own = chunk_of(self.chip_at(step))
            if step == chips // 2 - 1:
                own = jnp.concatenate(
                    [own[..., :half] + onward.astype(jnp.float32), own[..., half:]], axis=-1
                )
            else:
                own = own + onward.astype(jnp.float32)
            onward = lax.ppermute(own.astype(wire), AXIS, self.ahead)
            own = chunk_of(self.chip_at(-step))
            if step == chips // 2 - 1:
                own = jnp.concatenate(
                    [own[..., :half], own[..., half:] + backward.astype(jnp.float32)], axis=-1
                )
            else:
                own = own + backward.astype(jnp.float32)
            backward = lax.ppermute(own.astype(wire), AXIS, self.back)
        return chunk_of(self.chip) + onward.astype(jnp.float32) + backward.astype(jnp.float32)


def exchange_sum(value, axis, size, first=1):
    hop = first
    while hop < size:
        partner = [(device, device ^ hop) for device in range(size)]
        value = value + lax.ppermute(value, axis, partner)
        hop *= 2
    return value


def replica_sum(value, size, wire):
    hop = 1
    while hop < size:
        partner = [(device, device ^ hop) for device in range(size)]
        sent = value.astype(wire)
        value = sent.astype(jnp.float32) + lax.ppermute(sent, "replica", partner).astype(
            jnp.float32
        )
        hop *= 2
    return value


def masked_scores(keys, queries, key_seg, query_seg, diagonal):
    scores = matmul_nt(keys, queries) * (HEAD**-0.5)
    allowed = key_seg == query_seg
    if diagonal:
        key_at = lax.broadcasted_iota(jnp.int32, scores.shape, 0)
        query_at = lax.broadcasted_iota(jnp.int32, scores.shape, 1)
        allowed = allowed & (key_at <= query_at)
    return jnp.where(allowed, scores, NEGATIVE)


def attention_forward_kernel(
    chip_ref, q_ref, kv_ref, key_seg_ref, query_seg_ref, out_ref, lse_ref, top, total, mixed
):
    chip = chip_ref[0]
    rows = q_ref.shape[1]
    query_seg = query_seg_ref[...]
    top[...] = jnp.full(top.shape, NEGATIVE, jnp.float32)
    total[...] = jnp.zeros(total.shape, jnp.float32)
    mixed[...] = jnp.zeros(mixed.shape, jnp.float32)

    def block(at, diagonal):
        begin = pl.multiple_of(at * rows, rows)
        keys = kv_ref[0, pl.ds(begin, rows), :]
        values = kv_ref[1, pl.ds(begin, rows), :]
        key_seg = key_seg_ref[pl.ds(begin, rows), :]
        for head in range(GROUP):
            scores = masked_scores(keys, q_ref[head], key_seg, query_seg, diagonal)
            before = top[head : head + 1, :]
            now = jnp.maximum(before, jnp.max(scores, axis=0, keepdims=True))
            weights = jnp.where(scores > 0.5 * NEGATIVE, jnp.exp(scores - now), 0.0)
            shrink = jnp.exp(before - now)
            top[head : head + 1, :] = now
            total[head : head + 1, :] = total[head : head + 1, :] * shrink + jnp.sum(
                weights, axis=0, keepdims=True
            )
            mixed[head] = mixed[head] * shrink + matmul_tn(values, to_low(weights))

    lax.fori_loop(0, chip, lambda at, unused: (block(at, False), unused)[1], 0)
    block(chip, True)
    for head in range(GROUP):
        share = total[head : head + 1, :]
        lse_ref[head : head + 1, :] = top[head : head + 1, :] + jnp.log(share)
        out_ref[head] = to_low(mixed[head] / share)


def attention_backward_kernel(
    chip_ref,
    q_ref,
    do_ref,
    kv_ref,
    key_seg_ref,
    query_seg_ref,
    lse_ref,
    delta_ref,
    dq_ref,
    dkv_ref,
    dq_sum,
):
    chip = chip_ref[0]
    rows = q_ref.shape[1]
    query_seg = query_seg_ref[...]
    scale = HEAD**-0.5
    dq_sum[...] = jnp.zeros(dq_sum.shape, jnp.float32)

    def block(at, diagonal):
        begin = pl.multiple_of(at * rows, rows)
        keys = kv_ref[0, pl.ds(begin, rows), :]
        values = kv_ref[1, pl.ds(begin, rows), :]
        key_seg = key_seg_ref[pl.ds(begin, rows), :]
        dk = jnp.zeros((rows, HEAD), jnp.float32)
        dv = jnp.zeros((rows, HEAD), jnp.float32)
        for head in range(GROUP):
            queries, outs = q_ref[head], do_ref[head]
            scores = masked_scores(keys, queries, key_seg, query_seg, diagonal)
            weights = jnp.exp(scores - lse_ref[head : head + 1, :])
            d_weights = matmul_nt(values, outs)
            d_scores = to_low(weights * (d_weights - delta_ref[head : head + 1, :]))
            dk = dk + matmul(d_scores, queries)
            dv = dv + matmul(to_low(weights), outs)
            dq_sum[head] = dq_sum[head] + matmul_tn(keys, d_scores)
        dkv_ref[0, pl.ds(begin, rows), :] = dk * scale
        dkv_ref[1, pl.ds(begin, rows), :] = dv

    lax.fori_loop(0, chip, lambda at, unused: (block(at, False), unused)[1], 0)
    block(chip, True)

    def clear(at, unused):
        begin = pl.multiple_of(at * rows, rows)
        dkv_ref[:, pl.ds(begin, rows), :] = jnp.zeros((2, rows, HEAD), jnp.float32)
        return unused

    lax.fori_loop(chip + 1, kv_ref.shape[1] // rows, clear, 0)
    for head in range(GROUP):
        dq_ref[head] = to_low(dq_sum[head] * scale)


def in_smem():
    return pl.BlockSpec(memory_space=pltpu.SMEM)


def in_vmem():
    return pl.BlockSpec(memory_space=pltpu.VMEM)


def attention_forward(chip, queries, kv, key_seg, query_seg):
    rows = queries.shape[1]
    return pl.pallas_call(
        attention_forward_kernel,
        out_shape=(
            jax.ShapeDtypeStruct((GROUP, HEAD, rows), jnp.bfloat16),
            jax.ShapeDtypeStruct((GROUP, rows), jnp.float32),
        ),
        in_specs=[in_smem()] + [in_vmem()] * 4,
        out_specs=(in_vmem(), in_vmem()),
        scratch_shapes=[
            pltpu.VMEM((GROUP, rows), jnp.float32),
            pltpu.VMEM((GROUP, rows), jnp.float32),
            pltpu.VMEM((GROUP, HEAD, rows), jnp.float32),
        ],
        compiler_params=pltpu.CompilerParams(vmem_limit_bytes=40 * 2**20),
        name="attention_forward",
    )(chip, queries, kv, key_seg, query_seg)


def attention_backward(chip, queries, d_out, kv, key_seg, query_seg, lse, delta):
    rows = queries.shape[1]
    return pl.pallas_call(
        attention_backward_kernel,
        out_shape=(
            jax.ShapeDtypeStruct((GROUP, HEAD, rows), jnp.bfloat16),
            jax.ShapeDtypeStruct(kv.shape, jnp.float32),
        ),
        in_specs=[in_smem()] + [in_vmem()] * 7,
        out_specs=(in_vmem(), in_vmem()),
        scratch_shapes=[pltpu.VMEM((GROUP, HEAD, rows), jnp.float32)],
        compiler_params=pltpu.CompilerParams(vmem_limit_bytes=40 * 2**20),
        name="attention_backward",
    )(chip, queries, d_out, kv, key_seg, query_seg, lse, delta)


def decays(step_raw, decay_log, step_bias):
    step_size = jax.nn.softplus(step_raw + step_bias)
    cumulate = jnp.cumsum(-jnp.exp(decay_log) * step_size, axis=1)
    return (step_size, cumulate)


def ssm_summary(inputs, b_rows, step_raw, decay_log, step_bias, segment, previous):
    step_size, cumulate = decays(step_raw, decay_log, step_bias)
    carried_on = (segment == previous[:, None]).astype(jnp.float32)
    last_same = (segment == segment[:, -1:]).astype(jnp.float32)[:, :, None]
    weight_tail = jnp.exp(cumulate[:, -1:] - cumulate) * last_same * step_size
    weighted = inputs * weight_tail[..., None]
    fresh = jnp.einsum("kshp,ksn->khpn", weighted, b_rows, precision=HIGHEST)
    keep = jnp.exp(cumulate[:, -1]) * carried_on[:, -1:]
    chip_fresh, chip_keep = fresh[0], keep[0]
    for at in range(1, fresh.shape[0]):
        chip_fresh = keep[at][:, None, None] * chip_fresh + fresh[at]
        chip_keep = keep[at] * chip_keep
    return (chip_fresh, chip_keep, fresh, keep)


def ssm_output(
    state_in,
    fresh,
    keep,
    inputs,
    b_rows,
    c_rows,
    step_raw,
    decay_log,
    step_bias,
    skip_gain,
    gate_z,
    segment,
    previous,
):
    states = [state_in]
    for at in range(1, fresh.shape[0]):
        states.append(keep[at - 1][:, None, None] * states[-1] + fresh[at - 1])
    states = jnp.stack(states)
    step_size, cumulate = decays(step_raw, decay_log, step_bias)
    positions = jnp.arange(segment.shape[1])
    allowed = (segment[:, :, None] == segment[:, None, :]) & (
        positions[:, None] >= positions[None, :]
    )
    allowed_f = allowed.astype(jnp.float32)[:, None]
    by_head = cumulate.transpose(0, 2, 1)
    within = (
        jnp.exp(jnp.where(allowed[:, None], by_head[:, :, :, None] - by_head[:, :, None, :], 0.0))
        * allowed_f
    )
    cross_cb = jnp.einsum("ktn,ksn->kts", c_rows, b_rows, precision=HIGHEST)
    mixing = cross_cb[:, None] * within * step_size.transpose(0, 2, 1)[:, :, None, :]
    direct = jnp.einsum("khts,kshp->kthp", mixing, inputs, precision=HIGHEST)
    carried_on = (segment == previous[:, None]).astype(jnp.float32)
    entry_gain = jnp.exp(cumulate) * carried_on[:, :, None]
    carried = (
        jnp.einsum("khpn,ktn->kthp", states, c_rows, precision=HIGHEST) * entry_gain[..., None]
    )
    return (direct + carried + skip_gain[:, None] * inputs) * jax.nn.silu(gate_z)


def on_device(
    devices,
    replicas,
    tokens,
    segments,
    cotangent,
    norm_gain_one,
    in_weight,
    step_weight,
    qkv_weight,
    ssm_out_weight,
    attn_out_weight,
    decay_log,
    step_bias,
    skip_gain,
    norm_gain_two,
    gate_weight,
    up_weight,
    down_weight,
):
    ring = Ring(devices)
    chips, core, chip = ring.chips, ring.core, ring.chip
    first = core == 0
    tok_rows = tokens.shape[1]
    rows = SPLIT * tok_rows
    shard, width = in_weight.shape[0], tokens.shape[2]
    hidden = gate_weight.shape[1]
    slab = hidden // devices
    ff_here = hidden // SPLIT
    ssm_rows, attn_rows = ssm_out_weight.shape[0], attn_out_weight.shape[0]
    half_width = width // SPLIT
    ssm_width = SSM_HEADS * HEAD
    q_width, k_width = Q_HEADS * HEAD, KV_HEADS * HEAD
    q_here = GROUP * HEAD

    def mine(value, axis, which):
        size = value.shape[axis] // SPLIT
        return lax.dynamic_slice_in_dim(value, which * size, size, axis)

    def in_order(own, other, axis):
        return jnp.where(
            first,
            jnp.concatenate([own, other], axis=axis),
            jnp.concatenate([other, own], axis=axis),
        )

    def mixer_columns(which):
        ends = in_weight[:, 2 * ssm_width :]
        near = mine(ends, 1, which)
        far = mine(ends, 1, 1 - which)
        gains = jnp.stack([norm_gain_one, norm_gain_two], axis=1)
        extra = jnp.concatenate(
            [
                mine(step_weight, 1, which),
                gains,
                jnp.zeros((shard, EXTRA - HEADS_HERE - 2), jnp.bfloat16),
            ],
            axis=1,
        )
        return jnp.concatenate(
            [
                mine(in_weight[:, :ssm_width], 1, which),
                mine(in_weight[:, ssm_width : 2 * ssm_width], 1, which),
                near,
                far,
                mine(qkv_weight[:, :q_width], 1, which),
                mine(qkv_weight[:, q_width : q_width + k_width], 1, which),
                mine(qkv_weight[:, q_width + k_width :], 1, which),
                extra,
            ],
            axis=1,
        )

    mixer_own = in_order(mixer_columns(core), ring.swap(mixer_columns(1 - core)), 0)
    token_pair = in_order(tokens[0], ring.swap(tokens[0]), 0)
    upstream = in_order(cotangent[0], ring.swap(cotangent[0]), 0)
    w_mix = ring.gather(mixer_own).reshape(width, -1)

    out_shard = jnp.concatenate([ssm_out_weight, attn_out_weight], axis=0)
    out_shard = in_order(mine(out_shard, 1, core), ring.swap(mine(out_shard, 1, 1 - core)), 0)

    def ff_columns(which):
        parts = [
            lax.dynamic_index_in_dim(
                weight.reshape(shard, chips, SPLIT, slab), which, axis=2, keepdims=False
            ).reshape(shard, ff_here)
            for weight in (gate_weight, up_weight)
        ]
        return jnp.concatenate(parts, axis=1)

    ff_own = in_order(ff_columns(core), ring.swap(ff_columns(1 - core)), 0)

    seg_all = segments[0]
    first_row = chip * rows
    seg_mine = lax.dynamic_slice_in_dim(seg_all, first_row, rows)
    seg_blocks = seg_mine.reshape(SPLIT, tok_rows)
    before = jnp.where(
        first_row > 0,
        lax.dynamic_index_in_dim(seg_all, jnp.maximum(first_row - 1, 0), keepdims=False),
        -1,
    )
    seg_before = jnp.concatenate([before[None], seg_blocks[:-1, -1]])
    chip_scalar = chip.astype(jnp.int32).reshape(1)

    inputs = token_pair.astype(jnp.float32)
    extras = w_mix[:, -EXTRA:]
    gain_one = extras[:, HEADS_HERE].astype(jnp.float32)
    gain_two = extras[:, HEADS_HERE + 1].astype(jnp.float32)
    inverse_one = lax.rsqrt(jnp.mean(inputs * inputs, axis=-1, keepdims=True) + EPSILON)
    normed_one = inputs * inverse_one
    h_one = to_low(normed_one * gain_one)
    projected = matmul(h_one, w_mix)
    z_end, u_end = INNER, 2 * INNER
    near_end, far_end = u_end + STATE, u_end + 2 * STATE
    q_end = far_end + q_here
    k_end, v_end = q_end + HEAD, q_end + 2 * HEAD
    gate_z = projected[:, :z_end].reshape(SPLIT, tok_rows, HEADS_HERE, HEAD)
    ssm_x = projected[:, z_end:u_end].reshape(SPLIT, tok_rows, HEADS_HERE, HEAD)
    near, far = projected[:, u_end:near_end], projected[:, near_end:far_end]
    b_rows = jnp.where(first, near, far).reshape(SPLIT, tok_rows, STATE)
    c_rows = jnp.where(first, far, near).reshape(SPLIT, tok_rows, STATE)
    step_raw = projected[:, v_end : v_end + HEADS_HERE].reshape(SPLIT, tok_rows, HEADS_HERE)
    decay_here, bias_here, skip_here = (
        mine(decay_log, 0, core),
        mine(step_bias, 0, core),
        mine(skip_gain, 0, core),
    )

    kv_own = to_low(projected[:, q_end:v_end]).reshape(rows, 2, HEAD).transpose(1, 0, 2)
    kv_all = ring.gather(kv_own.reshape(2 * rows // 2, 2 * HEAD))
    kv_all = (
        kv_all.reshape(chips, 2, rows, HEAD).transpose(1, 0, 2, 3).reshape(2, chips * rows, HEAD)
    )

    summary_fn = partial(ssm_summary, segment=seg_blocks, previous=seg_before)
    (chip_fresh, chip_keep, fresh, keep), summary_back = jax.vjp(
        summary_fn, ssm_x, b_rows, step_raw, decay_here, bias_here
    )

    def pack_state(state, factor):
        tail = jnp.zeros((8, STATE), jnp.float32).at[0, :HEADS_HERE].set(factor)
        return jnp.concatenate([state.reshape(HEADS_HERE * HEAD, STATE), tail], axis=0)

    places = jnp.arange(chips, dtype=jnp.int32)

    def chained(packed, keeps, reverse):
        state = packed[:, : HEADS_HERE * HEAD].reshape(chips, HEADS_HERE, HEAD, STATE)
        total = jnp.zeros((HEADS_HERE,), jnp.float32)
        weights = [None] * chips
        running = jnp.ones((HEADS_HERE,), jnp.float32)
        for at in range(chips) if reverse else reversed(range(chips)):
            beyond = at > chip if reverse else at < chip
            weights[at] = jnp.where(beyond, running, 0.0)
            running = jnp.where(beyond, running * keeps[at], running)
        return jnp.einsum("kh,khpn->hpn", jnp.stack(weights), state, precision=HIGHEST)

    packed = ring.gather(pack_state(chip_fresh, chip_keep))
    keeps = packed[:, HEADS_HERE * HEAD, :HEADS_HERE]
    state_in = chained(packed, keeps, False)

    queries = to_low(projected[:, far_end:q_end]).reshape(rows, GROUP, HEAD).transpose(1, 0, 2)
    key_seg = seg_all[:, None]
    query_seg = seg_mine[None, :]
    attended_t, lse = attention_forward(chip_scalar, queries, kv_all, key_seg, query_seg)
    attended_low = attended_t.transpose(2, 0, 1).reshape(rows, q_here)

    output_fn = partial(ssm_output, segment=seg_blocks, previous=seg_before)
    gated, output_back = jax.vjp(
        output_fn,
        state_in,
        fresh,
        keep,
        ssm_x,
        b_rows,
        c_rows,
        step_raw,
        decay_here,
        bias_here,
        skip_here,
        gate_z,
    )
    gated_low = to_low(gated.reshape(rows, INNER))

    out_half = ring.gather(out_shard).reshape(chips * SPLIT, ssm_rows + attn_rows, half_width)
    out_ssm = out_half[:, :ssm_rows].reshape(devices * ssm_rows, half_width)
    out_attn = out_half[:, ssm_rows:].reshape(devices * attn_rows, half_width)

    def out_rows(which):
        return jnp.concatenate([mine(out_ssm, 0, which), mine(out_attn, 0, which)], axis=0)

    w_out = in_order(out_rows(core), ring.swap(out_rows(1 - core)), 1)
    mixed = jnp.concatenate([gated_low, attended_low], axis=1)
    branch = matmul(mixed, w_out)
    resid = inputs + (branch + ring.swap(branch))

    w_ff = ring.gather(ff_own).reshape(width, SPLIT * ff_here)
    w_down = ring.gather(down_weight).reshape(ff_here, width)
    inverse_two = lax.rsqrt(jnp.mean(resid * resid, axis=-1, keepdims=True) + EPSILON)
    normed_two = resid * inverse_two
    h_two = to_low(normed_two * gain_two)
    gate_up = matmul(h_two, w_ff)
    gate_pre, up_pre = gate_up[:, :ff_here], gate_up[:, ff_here:]
    sigmoid_gate = jax.nn.sigmoid(gate_pre)
    activated = to_low(gate_pre * sigmoid_gate * up_pre)
    partial_out = matmul(activated, w_down)
    result = (
        mine(resid, 0, core) + mine(partial_out, 0, core) + ring.swap(mine(partial_out, 0, 1 - core))
    )
    d_act = matmul_nt(upstream, w_down)
    d_gate = to_low(d_act * up_pre * sigmoid_gate * (1.0 + gate_pre * (1.0 - sigmoid_gate)))
    d_up = to_low(d_act * gate_pre * sigmoid_gate)
    d_gate_up = jnp.concatenate([d_gate, d_up], axis=1)
    d_h_two = matmul_nt(d_gate_up, w_ff)
    d_h_two = d_h_two + ring.swap(d_h_two)
    g_norm_two = 0.5 * jnp.sum(d_h_two * normed_two, axis=0)
    d_resid = upstream.astype(jnp.float32) + norm_back(d_h_two * gain_two, normed_two, inverse_two)
    d_branch = to_low(d_resid)

    def chunks(grad):
        pieces = grad.reshape((chips, -1) + grad.shape[1:])
        return lambda at: lax.dynamic_index_in_dim(pieces, at, keepdims=False)

    g_down = matmul_tn(activated, upstream)
    g_ff = matmul_tn(h_two, d_gate_up)
    down_sum = ring.scatter(chunks(g_down), jnp.bfloat16)
    ff_sum = ring.scatter(chunks(g_ff), jnp.bfloat16)

    d_mixed = matmul_nt(d_branch, w_out)
    d_gated = d_mixed[:, :INNER]
    d_att = to_low(d_mixed[:, INNER:])
    d_heads = d_att.reshape(rows, GROUP, HEAD).transpose(1, 0, 2)
    delta = jnp.sum(
        attended_low.astype(jnp.float32).reshape(rows, GROUP, HEAD)
        * d_att.astype(jnp.float32).reshape(rows, GROUP, HEAD),
        axis=-1,
    ).T
    dq_t, dkv = attention_backward(
        chip_scalar, queries, d_heads, kv_all, key_seg, query_seg, lse, delta
    )
    dkv_pieces = dkv.reshape(2, chips, rows, HEAD)

    def dkv_chunk(at):
        return lax.dynamic_index_in_dim(dkv_pieces, at, axis=1, keepdims=False).reshape(
            rows, 2 * HEAD
        )

    dkv_sum = ring.scatter(dkv_chunk, jnp.float32)
    dkv_low = to_low(dkv_sum.reshape(2, rows, HEAD).transpose(1, 0, 2).reshape(rows, 2 * HEAD))
    dq_low = dq_t.transpose(2, 0, 1).reshape(rows, q_here)

    grads_y = output_back(d_gated.reshape(SPLIT, tok_rows, HEADS_HERE, HEAD))
    later = ring.gather(pack_state(grads_y[0], chip_keep))
    later_grad = chained(later, keeps, True)
    grads_s = summary_back(
        (later_grad, jnp.sum(later_grad * state_in, axis=(1, 2)), grads_y[1], grads_y[2])
    )
    d_z = to_low(grads_y[10].reshape(rows, INNER))
    d_u = to_low((grads_y[3] + grads_s[0]).reshape(rows, INNER))
    d_b = (grads_y[4] + grads_s[1]).reshape(rows, STATE)
    d_c = grads_y[5].reshape(rows, STATE)
    d_near = to_low(jnp.where(first, d_b, d_c) + ring.swap(jnp.where(first, d_c, d_b)))
    d_step = to_low((grads_y[6] + grads_s[2]).reshape(rows, HEADS_HERE))
    head_grads = jnp.stack([grads_y[7] + grads_s[3], grads_y[8] + grads_s[4], grads_y[9]])
    d_step_wide = jnp.pad(d_step, ((0, 0), (0, EXTRA - HEADS_HERE)))
    d_projected = jnp.concatenate([d_z, d_u, d_near, dq_low, dkv_low, d_step_wide], axis=1)
    w_back = jnp.concatenate([w_mix[:, :near_end], w_mix[:, far_end:]], axis=1)

    g_out = matmul_tn(mixed, d_branch)
    g_mix = matmul_tn(h_one, d_projected)
    mix_sum = ring.scatter(chunks(g_mix), jnp.bfloat16)
    g_half = in_order(mine(g_out, 1, core), ring.swap(mine(g_out, 1, 1 - core)), 0)
    g_ssm = jnp.concatenate([g_half[:INNER], g_half[INNER + q_here : 2 * INNER + q_here]], axis=0)
    g_attn = jnp.concatenate([g_half[INNER : INNER + q_here], g_half[2 * INNER + q_here :]], axis=0)
    g_joint = jnp.concatenate(
        [
            g_ssm.reshape(devices, ssm_rows, half_width),
            g_attn.reshape(devices, attn_rows, half_width),
        ],
        axis=1,
    )
    out_sum = ring.scatter(
        chunks(g_joint.reshape(devices * (ssm_rows + attn_rows), half_width)), jnp.bfloat16
    )

    d_h_one = matmul_nt(d_projected, w_back)
    d_h_one = mine(d_h_one, 0, core) + ring.swap(mine(d_h_one, 0, 1 - core))
    normed_own = mine(normed_one, 0, core)
    g_norm_one = jnp.sum(d_h_one * normed_own, axis=0)
    d_inputs = mine(d_resid, 0, core) + norm_back(
        d_h_one * gain_one, normed_own, mine(inverse_one, 0, core)
    )

    def owned(total, axis=0):
        keep_part = mine(total, axis, core)
        other_part = ring.swap(mine(total, axis, 1 - core))
        return (
            jnp.where(first, keep_part, other_part),
            jnp.where(first, other_part, keep_part),
        )

    def whole(total):
        return replica_sum(total, replicas, jnp.bfloat16)

    down_grad = whole(down_sum)
    low_ff, high_ff = owned(whole(ff_sum))

    def interleave(low, high):
        return jnp.stack(
            [low.reshape(shard, chips, slab), high.reshape(shard, chips, slab)], axis=2
        ).reshape(shard, hidden)

    gate_grad = interleave(low_ff[:, :ff_here], high_ff[:, :ff_here])
    up_grad = interleave(low_ff[:, ff_here:], high_ff[:, ff_here:])
    low_out, high_out = owned(whole(out_sum))
    out_grad = jnp.concatenate([low_out, high_out], axis=1)
    low_mix, high_mix = owned(whole(mix_sum))

    def both(begin, end):
        return [low_mix[:, begin:end], high_mix[:, begin:end]]

    in_grad = jnp.concatenate(both(0, z_end) + both(z_end, u_end) + both(u_end, near_end), axis=1)
    q_at = near_end + q_here
    qkv_grad = jnp.concatenate(
        both(near_end, q_at) + both(q_at, q_at + HEAD) + both(q_at + HEAD, q_at + 2 * HEAD), axis=1
    )
    step_at = q_at + 2 * HEAD
    step_grad = jnp.concatenate(both(step_at, step_at + HEADS_HERE), axis=1)

    zeros = jnp.zeros_like(head_grads)
    head_wide = jnp.where(
        first,
        jnp.concatenate([head_grads, zeros], axis=1),
        jnp.concatenate([zeros, head_grads], axis=1),
    )
    small = jnp.concatenate([g_norm_one, g_norm_two, head_wide.reshape(-1)])
    small = exchange_sum(small, AXIS, devices)
    small = exchange_sum(small, "replica", replicas)
    index = lax.axis_index(AXIS)
    norm_one_grad = lax.dynamic_slice_in_dim(small, index * shard, shard)
    norm_two_grad = lax.dynamic_slice_in_dim(small, width + index * shard, shard)
    heads = small[2 * width :].reshape(3, SSM_HEADS)

    return (
        to_low(result)[None],
        to_low(d_inputs)[None],
        norm_one_grad,
        in_grad,
        step_grad,
        qkv_grad,
        out_grad[:ssm_rows],
        out_grad[ssm_rows:],
        heads[0],
        heads[1],
        heads[2],
        norm_two_grad,
        gate_grad,
        up_grad,
        down_grad,
    )


def solution(mesh):
    rows = P("fsdp", None)
    per_token = P("replica", "fsdp", None)
    vector = P("fsdp")
    return jax.shard_map(
        partial(on_device, mesh.shape["fsdp"], mesh.shape["replica"]),
        mesh=mesh,
        in_specs=(
            per_token,
            P("replica", None),
            per_token,
            vector,
            rows,
            rows,
            rows,
            rows,
            rows,
            P(),
            P(),
            P(),
            vector,
            rows,
            rows,
            rows,
        ),
        out_specs=(
            per_token,
            per_token,
            vector,
            rows,
            rows,
            rows,
            rows,
            rows,
            P(),
            P(),
            P(),
            vector,
            rows,
            rows,
            rows,
        ),
        check_vma=False,
    )
```

time: 1720 us -> 821 us (0.48)
  waiting for transfers between devices: 929 us -> 181 us
  matrix products: 371 us -> 109 us
  blocking collectives: 155 us -> 0 us
  starting transfers between devices: 0.8 us -> 150 us
  local copies, waits for them, and re-layouts: 109 us -> 232 us
  loops' own time: 18.7 us -> 0 us
    reduce_scatter x8 -> x0, waiting for transfers between devices: 628 us -> none  [the longest x1 146 us: on_device(): lax.psum_scatter(g_in, 'fsdp', scatter_dimension=0, tiled=True)]
    all_gather x10 -> x0, waiting for transfers between devices: 246 us -> none  [the longest x1 49.4 us: on_device(): lax.all_gather(gate_weight, 'fsdp', axis=0, tiled=True)]
    dot_general x84 -> x14, matrix products: 284 us -> 54 us  [the longest x3 26.2 us: ssm_output(): direct = jnp.einsum('khts,kshp->kthp', mixing, inputs, precision=HIGHEST)]
    ppermute x0 -> x120, waiting for transfers between devices: none -> 181 us  [the longest x21 48.2 us: gather(): onward = lax.ppermute(onward, AXIS, self.ahead)]
    ppermute x0 -> x120, starting transfers between devices: none -> 150 us  [the longest x15 32.2 us: scatter(): backward = lax.ppermute(own.astype(wire), AXIS, self.back)]
    dynamic_update_slice x16 -> x59, local copies, waits for them, and re-layouts: 8.32 us -> 91.1 us  [put(): lax.dynamic_update_slice(whole, part[None], (self.chip_at(offset),) + zer...]
    unnamed x2 -> x0, blocking collectives: 67.1 us -> none
    psum x1 -> x0, waiting for transfers between devices: 50.9 us -> none  [on_device(): lax.psum((mixer_grads[0], mixer_grads[1], mixer_grads[2], mixer_grads[3],...]
  transfers between devices with their start and end apart: 20 -> 120, of which waited for: 15 -> 38; matrix products, arithmetic and copies ran while one was open for 24% -> 51% of each run, Pallas kernels for 0% -> 1%
where the time goes in v1:
time: 821 us; the launch traced here: 808 us
  local copies, waits for them, and re-layouts  232 us (28%)
  waiting for transfers between devices  181 us (22%)
  starting transfers between devices  150 us (18%)
  matrix products  109 us (13%)
  other arithmetic  102 us (12%)
  between operations  28.4 us (3%)
    dynamic_update_slice x59, local copies, waits for them, and re-layouts, put(): lax.dynamic_update_slice(whole, part[None], (self.chip_at(offset),) + zer...  91.1 us
    ppermute x21, waiting for transfers between devices, gather(): onward = lax.ppermute(onward, AXIS, self.ahead)  48.2 us
    ppermute x15, starting transfers between devices, scatter(): backward = lax.ppermute(own.astype(wire), AXIS, self.back)  32.2 us
    ppermute x21, starting transfers between devices, gather(): onward = lax.ppermute(onward, AXIS, self.ahead)  30.8 us
    ppermute x15, waiting for transfers between devices, scatter(): onward = lax.ppermute(own.astype(wire), AXIS, self.ahead)  29.6 us
    ppermute x21, starting transfers between devices, gather(): backward = lax.ppermute(backward, AXIS, self.back)  26.7 us
    dot_general x3, matrix products, ssm_output(): direct = jnp.einsum('khts,kshp->kthp', mixing, inputs, precision=HIGHEST)  26.2 us
    ppermute x5, waiting for transfers between devices, scatter(): onward = lax.ppermute(far[..., :half].astype(wire), AXIS, self.ahead)  24.5 us
  transfers between devices with their start and end apart: 120, of which 38 were waited for; matrix products, arithmetic and copies ran while one was open for 51% of the time, Pallas kernels for 1%

profile of v1, /device:TPU:0, one launch (start us, length us, event | category | flops | bytes accessed | tf_op | source)
XLA Modules:
  0.0 807.8 jit_solution(1902892251117166920)
XLA Ops:
  73.6 10.6 %collective-permute-done.48 = bf16[128,1024]{1,0:T(8,128)(2,1)S(1)} collective-permute-done((bf16[128,1024]{1,0:T(8,128)(2,1)}, bf16[128,1024]{1,0:T(8,128)(2,1)S(1)}, u32[]{:S(2)}, u32[]{:S(2)}) %collective-permute-start.48) | collective-permute-done | bytes 262176 | tf_op jit(solution)/shard_map/ppermute | solution.py:107
  94.7 8.7 %collective-permute-done.30 = bf16[256,512]{1,0:T(8,128)(2,1)S(1)} collective-permute-done((bf16[256,512]{1,0:T(8,128)(2,1)S(1)}, bf16[256,512]{1,0:T(8,128)(2,1)S(1)}, u32[]{:S(2)}, u32[]{:S(2)}) %collective-permute-start.30) | collective-permute-done | bytes 262176 | tf_op jit(solution)/shard_map/ppermute | solution.py:108
  107.4 6.3 collective-permute-done.50
  122.1 7.9 collective-permute-done.3
  145.2 5.4 collective-permute-done.34
  157.3 9.4 %collective-permute-done.6 = bf16[128,2304]{1,0:T(8,128)(2,1)S(1)} collective-permute-done((bf16[128,2304]{1,0:T(8,128)(2,1)S(1)}, bf16[128,2304]{1,0:T(8,128)(2,1)S(1)}, u32[]{:S(2)}, u32[]{:S(2)}) %collective-permute-start.6) | collective-permute-done | bytes 589856 | tf_op jit(solution)/shard_map/ppermute | solution.py:107
  174.5 7.0 copy.460
  182.3 15.8 %dynamic_update_slice.197 = bf16[8,128,2304]{1,0,2:T(8,128)(2,1)} dynamic-update-slice(bf16[8,128,2304]{1,0,2:T(8,128)(2,1)} %copy.460, bf16[1,128,1152]{1,0,2:T(2,128)(2,1)S(1)} %copy.461, s32[]{:T(128)S(6)} %select_n.1076, s32[]{:T(128)} %constant.265.clone.1, s32[]{:T(128)} %constant.291.clone.1) | dynamic-update-slice | bytes 589828 | tf_op jit(solution)/shard_map/dynamic_update_slice | solution.py:100
  286.8 6.9 collective-permute-start.14
  301.6 7.1 collective-permute-start.16
  335.1 6.3 fusion.15
  344.8 8.5 %multiply_convert_fusion.5 = (bf16[2,256,12,64]{1,3,2,0:T(8,128)(2,1)S(1)}, f32[2,256,12,64]{1,3,2,0:T(8,128)}) fusion(f32[2,256,12,64]{1,0,3,2:T(2,128)S(1)} %copy-done.29, f32[2,256,12,64]{1,0,3,2:T(2,128)S(1)} %copy-done.5, f32[12]{0:T(128)S(1)} %copy-done.145, f32[2,256,12,64]{1,3,2,0:T(8,128)S(1)} %fusion.86, f32[2,256,12]{1,2,0:T(8,128)S(1)} %copy-done.80, ...), kind=kOutput, calls=%fused_computation.68 | convolution fusion | flops 1219756032 | bytes 8331312 | tf_op jit(solution)/shard_map/jvp(khts,kshp->kthp)/dot_general | solution.py:356
  386.6 5.3 fusion.155
  396.3 5.9 fusion.53
  425.1 5.1 collective-permute-done.112
  433.3 12.4 %collective-permute-done.113 = bf16[128,1024]{1,0:T(8,128)(2,1)S(1)} collective-permute-done((bf16[128,1024]{1,0:T(8,128)(2,1)S(1)}, bf16[128,1024]{1,0:T(8,128)(2,1)S(1)}, u32[]{:S(2)}, u32[]{:S(2)}) %collective-permute-start.113) | collective-permute-done | bytes 262176 | tf_op jit(solution)/shard_map/ppermute | solution.py:130
  458.2 6.6 collective-permute-done.103
  488.9 8.4 %fusion.110 = f32[512,1024]{1,0:T(8,128)S(1)} fusion(f32[512,1024]{1,0:T(8,128)S(1)} %multiply_add_fusion, bf16[1024,512]{1,0:T(8,128)(2,1)} %collective-permute-done.35, bf16[256,512]{1,0:T(8,128)(2,1)S(1)} %copy-done.84, bf16[768,512]{1,0:T(8,128)(2,1)S(1)} %copy-done.67, pred[]{:T(512)S(6)} %eq.59), kind=kOutput, calls=%fused_computation.222 | convolution fusion | flops 1087897600 | bytes 6291457 | tf_op jit(solution)/shard_map/dot_general | solution.py:42
  515.4 10.8 %fusion.12 = (f32[2,12,256]{2,1,0:T(8,128)S(1)}, f32[2,12,256]{2,1,0:T(8,128)}, f32[2,12,256]{2,1,0:T(8,128)}, f32[2,256,256]{2,1,0:T(8,128)}) fusion(f32[2,12,256]{2,1,0:T(8,128)S(1)} %copy-done.108, f32[2,256,256]{2,1,0:T(8,128)S(1)} %copy-done.71, f32[2,12,256]{2,1,0:T(8,128)S(1)} %copy-done.63, f32[2,256,256]{2,1,0:T(8,128)S(1)} %copy-done.74, ...), kind=kOutput, calls=%fused_computation.17 | convolution fusion | flops 1231403008 | bytes 4972544 | tf_op jit(solution)/shard_map/transpose(jvp(khts,kshp->kthp))/dot_general | solution.py:356
  549.9 5.0 reduce-window.24
  565.1 6.5 collective-permute-done.66
  571.5 7.7 collective-permute-start.71
  596.5 7.2 collective-permute-start.72
  631.1 7.1 collective-permute-done.61
  667.1 6.9 fusion.36
  678.2 5.0 reduce-window.26
  693.0 5.6 fusion.7
  706.6 7.0 collective-permute-done.80
  723.3 7.6 collective-permute-done.91
  741.5 11.0 %collective-permute-done.76 = f32[2120]{0:T(1024)S(1)} collective-permute-done((f32[2120]{0:T(1024)S(1)}, f32[2120]{0:T(1024)S(1)}, u32[]{:S(2)}, u32[]{:S(2)}) %collective-permute-start.76) | collective-permute-done | bytes 8512 | tf_op jit(solution)/shard_map/ppermute | solution.py:146
  780.9 7.5 collective-permute-done.98
  797.2 5.8 collective-permute-done.88
  (941 shorter events, 535.3 us)
Async XLA Ops:
  0.7 57.7 %collective-permute-start.46 = (bf16[128,1024]{1,0:T(8,128)(2,1)}, bf16[128,1024]{1,0:T(8,128)(2,1)}, u32[]{:S(2)}, u32[]{:S(2)}) collective-permute-start(bf16[128,1024]{1,0:T(8,128)(2,1)} %param.38), channel_id=1, source_target_pairs={{0,4},{1,5},{4,8},{5,9},{8,12},{9,13},{12,14},{13,15},{14,10},{15,... | collective-permute-start | bytes 786440 | tf_op jit(solution)/shard_map/ppermute | solution.py:107
  3.7 58.4 %collective-permute-start.47 = (bf16[128,1024]{1,0:T(8,128)(2,1)}, bf16[128,1024]{1,0:T(8,128)(2,1)}, u32[]{:S(2)}, u32[]{:S(2)}) collective-permute-start(bf16[128,1024]{1,0:T(8,128)(2,1)} %param.38), channel_id=1, source_target_pairs={{4,0},{5,1},{8,4},{9,5},{12,8},{13,9},{14,12},{15,13},{10,14},{11,... | collective-permute-start | bytes 786440 | tf_op jit(solution)/shard_map/ppermute | solution.py:108
  10.0 42.7 %collective-permute-start.37 = (bf16[64,2048]{1,0:T(8,128)(2,1)}, bf16[64,2048]{1,0:T(8,128)(2,1)}, u32[]{:S(2)}, u32[]{:S(2)}) collective-permute-start(bf16[64,2048]{1,0:T(8,128)(2,1)} %pad_maximum_fusion.19), channel_id=1, source_target_pairs={{0,1},{1,0},{2,3},{3,2},{4,5},{5,4},{6,7},{7,6},{8,9},{9,8},{10,11... | collective-permute-start | bytes 786440 | tf_op jit(solution)/shard_map/ppermute | solution.py:88
  13.4 50.4 %collective-permute-start.1 = (bf16[64,2304]{1,0:T(8,128)(2,1)}, bf16[64,2304]{1,0:T(8,128)(2,1)}, u32[]{:S(2)}, u32[]{:S(2)}) collective-permute-start(bf16[64,2304]{1,0:T(8,128)(2,1)} %concatenate.225), channel_id=1, source_target_pairs={{0,1},{1,0},{2,3},{3,2},{4,5},{5,4},{6,7},{7,6},{8,9},{9,8},{10,11... | collective-permute-start | bytes 884744 | tf_op jit(solution)/shard_map/ppermute | solution.py:88
  14.7 37.2 %collective-permute-start.26 = (bf16[128,512]{1,0:T(8,128)(2,1)}, bf16[128,512]{1,0:T(8,128)(2,1)S(1)}, u32[]{:S(2)}, u32[]{:S(2)}) collective-permute-start(bf16[128,512]{1,0:T(8,128)(2,1)} %get-tuple-element.257), channel_id=1, source_target_pairs={{0,1},{1,0},{2,3},{3,2},{4,5},{5,4},{6,7},{7,6},{8,9},{9,8},{10,11... | collective-permute-start | bytes 393224 | tf_op jit(solution)/shard_map/ppermute | solution.py:88
  51.9 35.8 %collective-permute-start = (bf16[256,1024]{1,0:T(8,128)(2,1)S(1)}, bf16[256,1024]{1,0:T(8,128)(2,1)S(1)}, u32[]{:S(2)}, u32[]{:S(2)}) collective-permute-start(bf16[256,1024]{1,0:T(8,128)(2,1)S(1)} %bitcast.727), channel_id=1, source_target_pairs={{0,1},{1,0},{2,3},{3,2},{4,5},{5,4},{6,7},{7,6},{8,9},{9,8},{10,11... | collective-permute-start | bytes 1572872 | tf_op jit(solution)/shard_map/ppermute | solution.py:88
  52.7 339.2 %collective-permute-start.55 = (bf16[256,1024]{1,0:T(8,128)(2,1)}, bf16[256,1024]{1,0:T(8,128)(2,1)}, u32[]{:S(2)}, u32[]{:S(2)}) collective-permute-start(bf16[256,1024]{1,0:T(8,128)(2,1)} %bitcast.128), channel_id=1, source_target_pairs={{0,1},{1,0},{2,3},{3,2},{4,5},{5,4},{6,7},{7,6},{8,9},{9,8},{10,11... | collective-permute-start | bytes 1572872 | tf_op jit(solution)/shard_map/ppermute | solution.py:88
  63.8 41.3 %collective-permute-start.38 = (bf16[128,2048]{1,0:T(8,128)(2,1)S(1)}, bf16[128,2048]{1,0:T(8,128)(2,1)}, u32[]{:S(2)}, u32[]{:S(2)}) collective-permute-start(bf16[128,2048]{1,0:T(8,128)(2,1)S(1)} %maximum_select_fusion.7), channel_id=1, source_target_pairs={{0,4},{1,5},{4,8},{5,9},{8,12},{9,13},{12,14},{13,15},{14,10},{15,... | collective-permute-start | bytes 1572872 | tf_op jit(solution)/shard_map/ppermute | solution.py:107
  84.2 33.1 %collective-permute-start.39 = (bf16[128,2048]{1,0:T(8,128)(2,1)S(1)}, bf16[128,2048]{1,0:T(8,128)(2,1)}, u32[]{:S(2)}, u32[]{:S(2)}) collective-permute-start(bf16[128,2048]{1,0:T(8,128)(2,1)S(1)} %maximum_select_fusion.7), channel_id=1, source_target_pairs={{4,0},{5,1},{8,4},{9,5},{12,8},{13,9},{14,12},{15,13},{10,14},{11,... | collective-permute-start | bytes 1572872 | tf_op jit(solution)/shard_map/ppermute | solution.py:108
  94.3 26.5 %collective-permute-start.2 = (bf16[128,2304]{1,0:T(8,128)(2,1)S(1)}, bf16[128,2304]{1,0:T(8,128)(2,1)S(1)}, u32[]{:S(2)}, u32[]{:S(2)}) collective-permute-start(bf16[128,2304]{1,0:T(8,128)(2,1)S(1)} %maximum_select_fusion.5), channel_id=1, source_target_pairs={{0,4},{1,5},{4,8},{5,9},{8,12},{9,13},{12,14},{13,15},{14,10},{15,... | collective-permute-start | bytes 1769480 | tf_op jit(solution)/shard_map/ppermute | solution.py:107
  209.7 40.8 %collective-permute-start.18 = (bf16[512,128]{1,0:T(8,128)(2,1)}, bf16[512,128]{1,0:T(8,128)(2,1)}, u32[]{:S(2)}, u32[]{:S(2)}) collective-permute-start(bf16[512,128]{1,0:T(8,128)(2,1)} %reshape.1107), channel_id=1, source_target_pairs={{0,4},{1,5},{4,8},{5,9},{8,12},{9,13},{12,14},{13,15},{14,10},{15,... | collective-permute-start | bytes 393224 | tf_op jit(solution)/shard_map/ppermute | solution.py:107
  210.5 42.3 %collective-permute-start.19 = (bf16[512,128]{1,0:T(8,128)(2,1)}, bf16[512,128]{1,0:T(8,128)(2,1)}, u32[]{:S(2)}, u32[]{:S(2)}) collective-permute-start(bf16[512,128]{1,0:T(8,128)(2,1)} %reshape.1107), channel_id=1, source_target_pairs={{4,0},{5,1},{8,4},{9,5},{12,8},{13,9},{14,12},{15,13},{10,14},{11,... | collective-permute-start | bytes 393224 | tf_op jit(solution)/shard_map/ppermute | solution.py:108
  234.6 33.1 %collective-permute-start.10 = (f32[776,128]{1,0:T(8,128)}, f32[776,128]{1,0:T(8,128)}, u32[]{:S(2)}, u32[]{:S(2)}) collective-permute-start(f32[776,128]{1,0:T(8,128)} %fusion.114), channel_id=1, source_target_pairs={{0,4},{1,5},{4,8},{5,9},{8,12},{9,13},{12,14},{13,15},{14,10},{15,... | collective-permute-start | bytes 1191944 | tf_op jit(solution)/shard_map/ppermute | solution.py:107
  235.5 33.6 %collective-permute-start.11 = (f32[776,128]{1,0:T(8,128)}, f32[776,128]{1,0:T(8,128)}, u32[]{:S(2)}, u32[]{:S(2)}) collective-permute-start(f32[776,128]{1,0:T(8,128)} %fusion.114), channel_id=1, source_target_pairs={{4,0},{5,1},{8,4},{9,5},{12,8},{13,9},{14,12},{15,13},{10,14},{11,... | collective-permute-start | bytes 1191944 | tf_op jit(solution)/shard_map/ppermute | solution.py:108
  273.3 40.0 %collective-permute-start.40 = (bf16[128,2048]{1,0:T(8,128)(2,1)}, bf16[128,2048]{1,0:T(8,128)(2,1)}, u32[]{:S(2)}, u32[]{:S(2)}) collective-permute-start(bf16[128,2048]{1,0:T(8,128)(2,1)} %collective-permute-done.38), channel_id=1, source_target_pairs={{0,4},{1,5},{4,8},{5,9},{8,12},{9,13},{12,14},{13,15},{14,10},{15,... | collective-permute-start | bytes 1572872 | tf_op jit(solution)/shard_map/ppermute | solution.py:107
  276.3 37.0 %collective-permute-start.41 = (bf16[128,2048]{1,0:T(8,128)(2,1)}, bf16[128,2048]{1,0:T(8,128)(2,1)}, u32[]{:S(2)}, u32[]{:S(2)}) collective-permute-start(bf16[128,2048]{1,0:T(8,128)(2,1)} %collective-permute-done.39), channel_id=1, source_target_pairs={{4,0},{5,1},{8,4},{9,5},{12,8},{13,9},{14,12},{15,13},{10,14},{11,... | collective-permute-start | bytes 1572872 | tf_op jit(solution)/shard_map/ppermute | solution.py:108
  313.3 40.9 %collective-permute-start.35 = (bf16[1024,512]{1,0:T(8,128)(2,1)}, bf16[1024,512]{1,0:T(8,128)(2,1)}, u32[]{:S(2)}, u32[]{:S(2)}) collective-permute-start(bf16[1024,512]{1,0:T(8,128)(2,1)} %pad_maximum_fusion.6), channel_id=1, source_target_pairs={{0,1},{1,0},{2,3},{3,2},{4,5},{5,4},{6,7},{7,6},{8,9},{9,8},{10,11... | collective-permute-start | bytes 3145736 | tf_op jit(solution)/shard_map/ppermute | solution.py:88
  313.3 49.5 %collective-permute-start.42 = (bf16[128,2048]{1,0:T(8,128)(2,1)}, bf16[128,2048]{1,0:T(8,128)(2,1)}, u32[]{:S(2)}, u32[]{:S(2)}) collective-permute-start(bf16[128,2048]{1,0:T(8,128)(2,1)} %collective-permute-done.40), channel_id=1, source_target_pairs={{0,4},{1,5},{4,8},{5,9},{8,12},{9,13},{12,14},{13,15},{14,10},{15,... | collective-permute-start | bytes 1572872 | tf_op jit(solution)/shard_map/ppermute | solution.py:107
  317.9 47.7 %collective-permute-start.43 = (bf16[128,2048]{1,0:T(8,128)(2,1)}, bf16[128,2048]{1,0:T(8,128)(2,1)}, u32[]{:S(2)}, u32[]{:S(2)}) collective-permute-start(bf16[128,2048]{1,0:T(8,128)(2,1)} %collective-permute-done.41), channel_id=1, source_target_pairs={{4,0},{5,1},{8,4},{9,5},{12,8},{13,9},{14,12},{15,13},{10,14},{11,... | collective-permute-start | bytes 1572872 | tf_op jit(solution)/shard_map/ppermute | solution.py:108
  423.3 25.4 %collective-permute-start.102 = (bf16[128,2048]{1,0:T(8,128)(2,1)S(1)}, bf16[128,2048]{1,0:T(8,128)(2,1)S(1)}, u32[]{:S(2)}, u32[]{:S(2)}) collective-permute-start(bf16[128,2048]{1,0:T(8,128)(2,1)S(1)} %pad_maximum_fusion.15), channel_id=1, source_target_pairs={{0,4},{1,5},{4,8},{5,9},{8,12},{9,13},{12,14},{13,15},{14,10},{15,... | collective-permute-start | bytes 1572872 | tf_op jit(solution)/shard_map/ppermute | solution.py:130
  432.8 24.7 %collective-permute-start.106 = (bf16[128,2048]{1,0:T(8,128)(2,1)}, bf16[128,2048]{1,0:T(8,128)(2,1)}, u32[]{:S(2)}, u32[]{:S(2)}) collective-permute-start(bf16[128,2048]{1,0:T(8,128)(2,1)} %pad_maximum_fusion.16), channel_id=1, source_target_pairs={{4,0},{5,1},{8,4},{9,5},{12,8},{13,9},{14,12},{15,13},{10,14},{11,... | collective-permute-start | bytes 1572872 | tf_op jit(solution)/shard_map/ppermute | solution.py:138
  450.7 30.8 %collective-permute-start.56 = (f32[512,1024]{1,0:T(8,128)}, f32[512,1024]{1,0:T(8,128)}, u32[]{:S(2)}, u32[]{:S(2)}) collective-permute-start(f32[512,1024]{1,0:T(8,128)} %fusion.53), channel_id=1, source_target_pairs={{0,1},{1,0},{2,3},{3,2},{4,5},{5,4},{6,7},{7,6},{8,9},{9,8},{10,11... | collective-permute-start | bytes 6291464 | tf_op jit(solution)/shard_map/ppermute | solution.py:88
  474.4 105.8 %collective-permute-start.104 = (bf16[128,2048]{1,0:T(8,128)(2,1)}, bf16[128,2048]{1,0:T(8,128)(2,1)}, u32[]{:S(2)}, u32[]{:S(2)}) collective-permute-start(bf16[128,2048]{1,0:T(8,128)(2,1)} %get-tuple-element.165), channel_id=1, source_target_pairs={{0,4},{1,5},{4,8},{5,9},{8,12},{9,13},{12,14},{13,15},{14,10},{15,... | collective-permute-start | bytes 1572872 | tf_op jit(solution)/shard_map/ppermute | solution.py:130
  480.0 100.2 %collective-permute-start.108 = (bf16[128,2048]{1,0:T(8,128)(2,1)}, bf16[128,2048]{1,0:T(8,128)(2,1)}, u32[]{:S(2)}, u32[]{:S(2)}) collective-permute-start(bf16[128,2048]{1,0:T(8,128)(2,1)} %fusion.75), channel_id=1, source_target_pairs={{4,0},{5,1},{8,4},{9,5},{12,8},{13,9},{14,12},{15,13},{10,14},{11,... | collective-permute-start | bytes 1572872 | tf_op jit(solution)/shard_map/ppermute | solution.py:138
  513.1 91.7 %collective-permute-start.57 = (f32[776,128]{1,0:T(8,128)}, f32[776,128]{1,0:T(8,128)}, u32[]{:S(2)}, u32[]{:S(2)}) collective-permute-start(f32[776,128]{1,0:T(8,128)} %fusion.115), channel_id=1, source_target_pairs={{0,4},{1,5},{4,8},{5,9},{8,12},{9,13},{12,14},{13,15},{14,10},{15,... | collective-permute-start | bytes 1191944 | tf_op jit(solution)/shard_map/ppermute | solution.py:107
  513.6 93.1 %collective-permute-start.58 = (f32[776,128]{1,0:T(8,128)}, f32[776,128]{1,0:T(8,128)}, u32[]{:S(2)}, u32[]{:S(2)}) collective-permute-start(f32[776,128]{1,0:T(8,128)} %fusion.115), channel_id=1, source_target_pairs={{4,0},{5,1},{8,4},{9,5},{12,8},{13,9},{14,12},{15,13},{10,14},{11,... | collective-permute-start | bytes 1191944 | tf_op jit(solution)/shard_map/ppermute | solution.py:108
  582.0 36.0 %collective-permute-start.109 = (bf16[128,2048]{1,0:T(8,128)(2,1)S(1)}, bf16[128,2048]{1,0:T(8,128)(2,1)}, u32[]{:S(2)}, u32[]{:S(2)}) collective-permute-start(bf16[128,2048]{1,0:T(8,128)(2,1)S(1)} %fusion.79), channel_id=1, source_target_pairs={{0,16},{16,0},{1,17},{17,1},{2,18},{18,2},{3,19},{19,3},{4,20},{20... | collective-permute-start | bytes 1572872 | tf_op jit(solution)/shard_map/ppermute | solution.py:156
  595.5 120.9 %collective-permute-start.90 = (f32[1024,512]{1,0:T(8,128)}, f32[1024,512]{1,0:T(8,128)}, u32[]{:S(2)}, u32[]{:S(2)}) collective-permute-start(f32[1024,512]{1,0:T(8,128)} %get-tuple-element.190), channel_id=1, source_target_pairs={{0,1},{1,0},{2,3},{3,2},{4,5},{5,4},{6,7},{7,6},{8,9},{9,8},{10,11... | collective-permute-start | bytes 6291464 | tf_op jit(solution)/shard_map/ppermute | solution.py:88
  699.8 32.2 %collective-permute-start.74 = (f32[256,1024]{1,0:T(8,128)}, f32[256,1024]{1,0:T(8,128)S(1)}, u32[]{:S(2)}, u32[]{:S(2)}) collective-permute-start(f32[256,1024]{1,0:T(8,128)} %constant_dynamic-slice_fusion.5), channel_id=1, source_target_pairs={{0,1},{1,0},{2,3},{3,2},{4,5},{5,4},{6,7},{7,6},{8,9},{9,8},{10,11... | collective-permute-start | bytes 3145736 | tf_op jit(solution)/shard_map/ppermute | solution.py:88
  714.5 38.0 %collective-permute-start.85 = (bf16[128,2176]{1,0:T(8,128)(2,1)S(1)}, bf16[128,2176]{1,0:T(8,128)(2,1)S(1)}, u32[]{:S(2)}, u32[]{:S(2)}) collective-permute-start(bf16[128,2176]{1,0:T(8,128)(2,1)S(1)} %pad_maximum_fusion.14), channel_id=1, source_target_pairs={{4,0},{5,1},{8,4},{9,5},{12,8},{13,9},{14,12},{15,13},{10,14},{11,... | collective-permute-start | bytes 1671176 | tf_op jit(solution)/shard_map/ppermute | solution.py:138
  733.3 33.5 %collective-permute-start.96 = (bf16[256,512]{1,0:T(8,128)(2,1)}, bf16[256,512]{1,0:T(8,128)(2,1)}, u32[]{:S(2)}, u32[]{:S(2)}) collective-permute-start(bf16[256,512]{1,0:T(8,128)(2,1)} %pad_maximum_fusion.23), channel_id=1, source_target_pairs={{4,0},{5,1},{8,4},{9,5},{12,8},{13,9},{14,12},{15,13},{10,14},{11,... | collective-permute-start | bytes 786440 | tf_op jit(solution)/shard_map/ppermute | solution.py:138
  741.1 25.7 %collective-permute-start.93 = (bf16[256,512]{1,0:T(8,128)(2,1)}, bf16[256,512]{1,0:T(8,128)(2,1)}, u32[]{:S(2)}, u32[]{:S(2)}) collective-permute-start(bf16[256,512]{1,0:T(8,128)(2,1)} %fusion.105), channel_id=1, source_target_pairs={{0,4},{1,5},{4,8},{5,9},{8,12},{9,13},{12,14},{13,15},{14,10},{15,... | collective-permute-start | bytes 786440 | tf_op jit(solution)/shard_map/ppermute | solution.py:130
  (242 other events, 2962.2 us)
